TPU v7x, 512 devices: a whole 4x4x16 slice. The times are simulated.
512 devices in a mesh: dx: 32 (over z_lo, y), dy: 16 (over x, z_hi, core).
Axes of the slice: x: 4, y: 4, z: 16 (z_hi: 2, z_lo: 8; z = z_hi * 8 + z_lo), core: 2. Of those that a mesh axis runs over, the one named last changes fastest.
Arguments:
- query_hidden: bfloat16 [8192, 4096], P(('dx', 'dy')), as said below
- passage_hidden: bfloat16 [65536, 4096], P(('dx', 'dy')), as said below
- gain: float32 [4096], replicated, may hold values from 0.5 to 1.5
- hard_ids: int32 [8192, 7], P(('dx', 'dy')), may hold values from 0 to 4095, as said below
- positive_ids: int32 [8192], P(('dx', 'dy')), may hold values from 0 to 4095, as said below
Outputs:
- query_grad: bfloat16 [8192, 4096], P(('dx', 'dy'))
- passage_grad: bfloat16 [65536, 4096], P(('dx', 'dy'))
- gain_grad: float32 [4096], replicated
- loss: float32 [], replicated
Inputs may be any that keep to these rules, and one draw needn't show every extreme that they name: `query_hidden`: final-layer hidden states of order one. `passage_hidden`: final-layer hidden states of order one. `hard_ids`: the query of row r of device x of a group owns the 8 passage positions x * 128 + 8 * r to x * 128 + 8 * r + 7; its positive and its 7 hard negatives are these positions, each once. `positive_ids`: one of the query's own passage positions, as described for hard_ids.
All inputs are finite; a program needn't handle non-finite values.
Results may differ from a plain program's by a relative error of at most 0.017.
Values may be sent and summed in bfloat16 or wider, within the bound.
A program may use at most 64 MiB of HBM per device.

v0:
```python
import jax
import jax.numpy as jnp
from jax import lax
from jax.sharding import PartitionSpec as P

logit_scale = 250.0
hard_weight = 3.0


def embed(hidden, gain):
    values = hidden.astype(jnp.float32)
    inv_rms = lax.rsqrt(jnp.mean(values * values, axis=-1, keepdims=True) + 1e-05)
    unit = values * inv_rms
    normed = unit * gain
    inv_len = lax.rsqrt(jnp.sum(normed * normed, axis=-1, keepdims=True) + 1e-06)
    return ((normed * inv_len).astype(jnp.bfloat16), unit, normed, inv_len, inv_rms)


def backward(dembed, unit, normed, inv_len, inv_rms, gain):
    unit_embed = normed * inv_len
    dnormed = inv_len * (dembed - unit_embed * jnp.sum(unit_embed * dembed, axis=-1, keepdims=True))
    gain_part = jnp.sum(dnormed * unit, axis=0)
    dunit = dnormed * gain
    grad = inv_rms * (dunit - unit * jnp.mean(dunit * unit, axis=-1, keepdims=True))
    return (grad.astype(jnp.bfloat16), gain_part)


def score_block(queries, passages):
    return logit_scale * lax.dot_general(
        queries, passages, (((1,), (1,)), ((), ())), preferred_element_type=jnp.float32
    )


def on_device(query_hidden, passage_hidden, gain, hard_ids, positive_ids):
    q_dev = query_hidden.shape[0]
    p_dev = passage_hidden.shape[0]
    group_q = q_dev * lax.axis_size("dx")
    q_emb, q_unit, q_normed, q_inv, q_rms = embed(query_hidden, gain)
    p_emb, p_unit, p_normed, p_inv, p_rms = embed(passage_hidden, gain)
    x_index = lax.axis_index("dx")
    row_start = x_index * q_dev
    zero_col = jnp.zeros((), jnp.int32)
    hard_group = lax.dynamic_update_slice(
        jnp.full((group_q, hard_ids.shape[1]), -1, jnp.int32), hard_ids, (row_start, zero_col)
    )
    pos_group = lax.dynamic_update_slice(
        jnp.full((group_q,), -1, jnp.int32), positive_ids, (row_start,)
    )
    q_group = lax.all_gather(q_emb, "dx", axis=0, tiled=True)
    scores = score_block(q_group, p_emb)
    col_ids = x_index * p_dev + jnp.arange(p_dev, dtype=jnp.int32)
    counts = jnp.zeros(scores.shape, jnp.float32)
    for k in range(hard_group.shape[1]):
        counts = counts + (hard_group[:, k : k + 1] == col_ids[None, :]).astype(jnp.float32)
    weights = 1.0 + hard_weight * counts
    is_pos = pos_group[:, None] == col_ids[None, :]
    local_max = jnp.max(scores, axis=1)
    pos_part = jnp.sum(jnp.where(is_pos, scores, 0.0), axis=1)
    top = lax.pmax(local_max, "dx")
    local_sum = jnp.sum(weights * jnp.exp(scores - top[:, None]), axis=1)
    total, pos_score = lax.psum((local_sum, pos_part), "dx")
    log_total = top + jnp.log(total)
    dscore = (weights * jnp.exp(scores - log_total[:, None]) - is_pos.astype(jnp.float32)).astype(
        jnp.bfloat16
    )
    dq_own = lax.psum_scatter(
        (logit_scale * jnp.dot(dscore, p_emb, preferred_element_type=jnp.float32)).astype(
            jnp.bfloat16
        ),
        "dx",
        scatter_dimension=0,
        tiled=True,
    ).astype(jnp.float32)
    dp_own = logit_scale * lax.dot_general(
        dscore, q_group, (((0,), (0,)), ((), ())), preferred_element_type=jnp.float32
    )
    own_log = lax.dynamic_slice_in_dim(log_total, row_start, q_dev, 0)
    own_pos = lax.dynamic_slice_in_dim(pos_score, row_start, q_dev, 0)
    loss_part = jnp.sum(own_log - own_pos)
    query_grad, q_gain = backward(dq_own, q_unit, q_normed, q_inv, q_rms, gain)
    passage_grad, p_gain = backward(dp_own, p_unit, p_normed, p_inv, p_rms, gain)
    gain_grad, loss = lax.psum((q_gain + p_gain, loss_part), ("dx", "dy"))
    return (query_grad, passage_grad, gain_grad, loss)


def solution(mesh):
    placed = (
        P(("dx", "dy"), None),
        P(("dx", "dy"), None),
        P(),
        P(("dx", "dy"), None),
        P(("dx", "dy")),
    )
    return jax.shard_map(
        on_device,
        mesh=mesh,
        in_specs=placed,
        out_specs=(P(("dx", "dy"), None), P(("dx", "dy"), None), P(), P()),
        check_vma=False,
    )
```

profile of v0, /device:TPU:1, one launch (start us, length us, event | category | flops | bytes accessed | tf_op | source)
XLA Modules:
  0.0 839.9 jit_solution(7585294088920323583)
XLA Ops:
  7.2 0.0 copy-start.2
  7.2 0.0 copy-start
  7.2 0.0 all-gather.2.cloned.1.call-start
  7.2 1.1 fusion.33
  8.4 1.1 fusion.27
  9.5 1.7 fusion.26
  11.2 0.0 all-gather.2.cloned.1.call-update
  11.2 0.0 reduce-scatter.2.cloned.1.call-start
  11.3 0.9 dynamic_update_slice.9
  12.1 0.8 dynamic_update_slice.8
  12.9 1.5 fusion.18
  14.5 0.0 copy-done
  14.5 1.2 fusion.12
  15.7 209.2 %all-gather.2.cloned.1.call-done = bf16[512,4096]{1,0:T(8,128)(2,1)} async-done(((bf16[16,4096]{1,0:T(8,128)(2,1)}), bf16[512,4096]{1,0:T(8,128)(2,1)}) %all-gather.2.cloned.1.call-update) | async-done | bytes 4194320 | tf_op jit(solution)/shard_map/all_gather | solution.py:49
  224.9 0.0 copy-done.2
  224.9 3.7 fusion.44
  228.6 107.0 %pmax.7 = f32[512]{0:T(512)S(1)} all-reduce(f32[512]{0:T(512)S(1)} %get-tuple-element.21), channel_id=1, replica_groups=mesh['dx'=32,'dy'=16] {'dx'}, use_global_device_ids=true, to_apply=%region_5.6 | all-reduce | flops 512 | bytes 4096 | tf_op jit(solution)/shard_map/pmax | solution.py:59
  335.6 0.3 fusion.38
  335.9 98.9 %all-reduce.1 = (f32[512]{0:T(512)S(1)}, f32[512]{0:T(512)S(1)}) all-reduce(f32[512]{0:T(512)S(1)} %get-tuple-element.9, f32[512]{0:T(512)S(1)} %get-tuple-element.8), channel_id=1, replica_groups=mesh['dx'=32,'dy'=16] {'dx'}, use_global_device_ids=true, to_apply=%region_7.8 | all-reduce | flops 1024 | bytes 8192 | tf_op jit(solution)/shard_map/psum | solution.py:61
  434.8 3.6 multiply_convert_fusion
  438.4 0.0 reduce-scatter.2.cloned.1.call-update
  438.4 0.7 subtract_reduce_fusion
  439.1 3.7 fusion.9
  442.7 1.0 fusion.17
  443.8 0.0 copy-start.1
  443.8 2.0 fusion.16
  445.7 258.0 %reduce-scatter.2.cloned.1.call-done = bf16[16,4096]{1,0:T(8,128)(2,1)} async-done(((bf16[512,4096]{1,0:T(8,128)(2,1)}), bf16[16,4096]{1,0:T(8,128)(2,1)}) %reduce-scatter.2.cloned.1.call-update) | async-done | bytes 131088 | tf_op jit(solution)/shard_map/reduce_scatter | solution.py:66
  703.8 0.0 copy-done.1
  703.8 1.1 fusion.34
  704.9 1.2 fusion.32
  706.2 125.2 %all-reduce = (f32[4096]{0:T(1024)}, f32[]{:T(128)}) all-reduce(f32[4096]{0:T(1024)S(1)} %add.112, f32[]{:T(128)} %subtract_reduce_fusion), channel_id=1, replica_groups=mesh['dx'=32,'dy'=16] {'dx','dy'}, use_global_device_ids=true, to_apply=%region_15.16 | all-reduce | flops 4097 | bytes 32776 | tf_op jit(solution)/shard_map/psum | solution.py:82
  831.4 1.7 fusion.31
  (12 shorter events, 0.1 us)
Async XLA Ops:
  7.2 217.7 %copy-start.2 = (f32[4096]{0:T(1024)S(1)}, f32[4096]{0:T(1024)}, u32[]{:S(2)}) copy-start(f32[4096]{0:T(1024)} %param.7) | copy-start | bytes 49156
  7.2 7.3 copy-start
  7.2 217.7 %all-gather.2.cloned.1.call-start = ((), (), s32[]{:S(2)}) async-start(), calls=%async_computation.1 | async-start | bytes 4325376 | tf_op jit(solution)/shard_map/all_gather | solution.py:49
  11.2 692.6 %reduce-scatter.2.cloned.1.call-start = ((), (), s32[]{:S(2)}) async-start(), calls=%async_computation.2 | async-start | bytes 4325376 | tf_op jit(solution)/shard_map/reduce_scatter | solution.py:66
  443.8 260.0 %copy-start.1 = (bf16[16,4096]{1,0:T(8,128)(2,1)S(1)}, bf16[16,4096]{1,0:T(8,128)(2,1)}, u32[]{:S(2)}) copy-start(bf16[16,4096]{1,0:T(8,128)(2,1)} %param.5) | copy-start | bytes 393220
Sparse Core Ops, SparseCore 0:
  11.3 213.5 all-gather.1
  438.5 265.1 reduce-scatter.1
where the time goes:
time: 840 us
  waiting for transfers between devices  467 us (56%)
  blocking collectives  331 us (39%)
  other arithmetic  14.8 us (2%)
  between operations  14.1 us (2%)
  matrix products  11 us (1%)
    reduce_scatter x1, waiting for transfers between devices, on_device(): lax.psum_scatter((logit_scale * jnp.dot(dscore, p_emb, preferred_element_...  258 us
    all_gather x1, waiting for transfers between devices, on_device(): q_group = lax.all_gather(q_emb, 'dx', axis=0, tiled=True)  209 us
    psum x1, blocking collectives, on_device(): gain_grad, loss = lax.psum((q_gain + p_gain, loss_part), ('dx', 'dy'))  125 us
    pmax x1, blocking collectives, on_device(): top = lax.pmax(local_max, 'dx')  107 us
    psum x1, blocking collectives, on_device(): total, pos_score = lax.psum((local_sum, pos_part), 'dx')  98.9 us
  transfers between devices with their start and end apart: 2, of which 2 were waited for; matrix products, arithmetic and copies ran while one was open for 1% of the time, Pallas kernels for 0%

commit v1 on v0

v1 whole, which is shorter than its diff:
```python
import jax
import jax.numpy as jnp
from jax import lax
from jax.experimental import pallas as pl
from jax.experimental.pallas import tpu as pltpu
from jax.sharding import PartitionSpec as P

MESH = pl.DeviceIdType.MESH
F32 = jnp.float32
BF16 = jnp.bfloat16

LOGIT_SCALE = 250.0
HARD_WEIGHT = 3.0
D = 4096
QB = 16
PB = 128
RING = 8
CLASS = 16
NQ = QB * CLASS
NP = 2 * PB
NF = 4
FC = D // NF
SEG = D // CLASS


def kernel(
    q_ref, p_ref, gain_ref, pos_ref,
    qg_ref, pg_ref, gg_ref, loss_ref,
    qb, pb, sc, ds, dq, yr, zs, zr, dp, dps, dpr, dfin, pstat, stats, ga, gar, gb, gbr, gc, gd,
    agz_s, agz_r, agy_s, agy_r, px_s, px_r, st_s, st_r, rsy_s, rsy_r, rsz_s, rsz_r, dp_s, dp_r,
    ga_s, ga_r, gb_s, gb_r, gc_s, gc_r, gd_s, gd_r,
):
    dx = lax.axis_index("dx")
    dy = lax.axis_index("dy")
    y = dx % 4
    z = dx // 4
    half = z // 2
    r = half + (z % 2) * (7 - 2 * half)
    c = y // 2
    cls = (y + c) % 2
    ci = c * RING + r

    def z_of(place):
        return 2 * place + (place // 4) * (15 - 4 * place)

    nxt = z_of((r + 1) % RING) * 4 + y
    yp = z * 4 + 3 - y
    pp = z * 4 + y + 1 - 2 * (y % 2)

    def peer(k):
        other = (ci + k) % CLASS
        c2 = other // RING
        return z_of(other % RING) * 4 + cls + c2 * (3 - 2 * cls)

    def rows(block, size=QB):
        return pl.ds(pl.multiple_of(block * size, size), size)

    def remote(src, dst, send, recv, dev):
        return pltpu.make_async_remote_copy(
            src_ref=src, dst_ref=dst, send_sem=send, recv_sem=recv, device_id=dev, device_id_type=MESH
        )

    barrier = pltpu.get_barrier_semaphore()

    def greet(k, _):
        pl.semaphore_signal(barrier, inc=1, device_id=(peer(k), dy), device_id_type=MESH)
        pl.semaphore_signal(barrier, inc=1, device_id=(dx, (dy + k) % 16), device_id_type=MESH)
        return 0

    lax.fori_loop(1, 16, greet, 0)
    pl.semaphore_signal(barrier, inc=1, device_id=(pp, dy), device_id_type=MESH)

    def embed(hidden):
        v = hidden.astype(F32)
        vg = v * gain_ref[...]
        inv_rms = lax.rsqrt(jnp.sum(v * v, axis=1, keepdims=True) * (1.0 / D) + 1e-05)
        inv_len = lax.rsqrt(jnp.sum(vg * vg, axis=1, keepdims=True) * (inv_rms * inv_rms) + 1e-06)
        return v, vg * (inv_rms * inv_len), inv_rms, inv_len

    _, q_e, _, _ = embed(q_ref[...])
    for f in range(NF):
        qb[f, rows(ci), :] = q_e[:, f * FC:(f + 1) * FC].astype(BF16)

    pl.semaphore_wait(barrier, 31)

    def agz(s, f):
        block = qb.at[f, rows(c * RING + (r - s + RING) % RING), :]
        return remote(block, block, agz_s.at[s, f], agz_r.at[s + 1, f], (nxt, dy))

    def agz_got(s, f):
        block = qb.at[f, rows(c * RING + (r - s + RING) % RING), :]
        return remote(block, block, agz_s.at[s, f], agz_r.at[s, f], (nxt, dy))

    def agy(s, f):
        block = qb.at[f, rows(c * RING + (r - s + RING) % RING), :]
        return remote(block, block, agy_s.at[s, f], agy_r.at[s, f], (yp, dy))

    def agy_got(s, f):
        block = qb.at[f, rows((1 - c) * RING + (r - s + RING) % RING), :]
        return remote(block, block, agy_s.at[s, f], agy_r.at[s, f], (yp, dy))

    for f in range(NF):
        agz(0, f).start()
        agy(0, f).start()

    def embed_block(b, _):
        _, e, inv_rms, inv_len = embed(p_ref[rows(b), :])
        for f in range(NF):
            pb[f, rows(b), :] = e[:, f * FC:(f + 1) * FC].astype(BF16)
        pstat[0, rows(b), :] = inv_rms
        pstat[1, rows(b), :] = inv_len
        return 0

    lax.fori_loop(0, PB // QB, embed_block, 0)

    def swap(f):
        return remote(pb.at[f, pl.ds(0, PB), :], pb.at[f, pl.ds(PB, PB), :], px_s.at[f], px_r.at[f], (pp, dy))

    for f in range(NF):
        swap(f).start()

    def ag_step(s, _):
        for f in range(NF):
            agz_got(s, f).wait_recv()
            agz(s, f).start()
            agy(s, f).start()
        return 0

    lax.fori_loop(1, RING - 1, ag_step, 0)
    for f in range(NF):
        agz_got(RING - 1, f).wait_recv()
        agy(RING - 1, f).start()

    for f in range(NF):
        def got(s, _, f=f):
            agy_got(s, f).wait_recv()
            return 0

        lax.fori_loop(0, RING, got, 0)
        swap(f).wait_recv()
        part = lax.dot_general(pb[f], qb[f], (((1,), (1,)), ((), ())), preferred_element_type=F32)
        sc[...] = part if f == 0 else sc[...] + part
    sc[...] = sc[...] * LOGIT_SCALE

    lane = lax.broadcasted_iota(jnp.int32, (PB, NQ), 1)
    row = lax.broadcasted_iota(jnp.int32, (PB, NQ), 0)
    own = (lane == ci * QB + row // 8).astype(F32)
    ids = lax.broadcasted_iota(jnp.int32, (PB, QB), 0) + dx * PB
    flag = jnp.sum((ids == pos_ref[...]).astype(F32), axis=1, keepdims=True)
    is_pos = own * flag
    weights = 1.0 + HARD_WEIGHT * (own - is_pos)

    s_own = sc[0:PB, :]
    s_far = sc[PB:NP, :]
    top = jnp.maximum(jnp.max(s_own, axis=0, keepdims=True), jnp.max(s_far, axis=0, keepdims=True))
    total = jnp.sum(weights * jnp.exp(s_own - top), axis=0, keepdims=True) + jnp.sum(
        jnp.exp(s_far - top), axis=0, keepdims=True
    )
    stats[ci, 0:1, :] = top
    stats[ci, 1:2, :] = total

    def stat(k):
        return remote(stats.at[ci], stats.at[ci], st_s.at[k], st_r.at[k], (peer(k), dy))

    def stat_got(k):
        slot = stats.at[(ci - k + CLASS) % CLASS]
        return remote(slot, slot, st_s.at[k], st_r.at[k], (peer(k), dy))

    def start_stat(k, _):
        stat(k).start()
        return 0

    def wait_stat(k, _):
        stat_got(k).wait_recv()
        return 0

    lax.fori_loop(1, CLASS, start_stat, 0)
    pos_score = jnp.sum(is_pos * s_own, axis=0, keepdims=True)
    lax.fori_loop(1, CLASS, wait_stat, 0)
    top_all = stats[0, 0:1, :]
    for k in range(1, CLASS):
        top_all = jnp.maximum(top_all, stats[k, 0:1, :])
    sum_all = jnp.zeros((1, NQ), F32)
    for k in range(CLASS):
        sum_all = sum_all + stats[k, 1:2, :] * jnp.exp(stats[k, 0:1, :] - top_all)
    log_total = top_all + jnp.log(sum_all)
    lane1 = lax.broadcasted_iota(jnp.int32, (1, NQ), 1)
    loss_part = jnp.sum(
        jnp.where(lane1 // QB == ci, log_total - pos_score, 0.0), axis=1, keepdims=True
    )

    ds[0:PB, :] = (weights * jnp.exp(s_own - log_total) - is_pos).astype(BF16)
    ds[PB:NP, :] = jnp.exp(s_far - log_total).astype(BF16)
    ds_f = ds[...].astype(F32)
    ds_t = jnp.transpose(ds_f).astype(BF16)
    prod = ds_f * sc[...]
    u = jnp.sum(prod, axis=1, keepdims=True)
    t_row = jnp.sum(prod, axis=0, keepdims=True)
    t = jnp.transpose(jnp.broadcast_to(t_row, (8, NQ)))[:, 0:1]

    def dest(j):
        return (r + 2 * RING - 1 - j) % RING

    def rsy(j, f):
        return remote(
            dq.at[f, rows((1 - c) * RING + dest(j)), :], yr.at[j, f], rsy_s.at[j, f], rsy_r.at[j, f], (yp, dy)
        )

    def rsz(j, f):
        return remote(zs.at[j, f], zr.at[j + 1, f], rsz_s.at[j, f], rsz_r.at[j + 1, f], (nxt, dy))

    def rsz_got(j, f):
        return remote(zs.at[j, f], zr.at[j, f], rsz_s.at[j, f], rsz_r.at[j, f], (nxt, dy))

    def send_dp(f):
        return remote(dps.at[f], dpr.at[f], dp_s.at[f], dp_r.at[f], (pp, dy))

    for f in range(NF):
        dq[f] = (LOGIT_SCALE * jnp.dot(ds_t, pb[f], preferred_element_type=F32)).astype(BF16)

        def start_rsy(j, _, f=f):
            rsy(j, f).start()
            return 0

        lax.fori_loop(0, RING, start_rsy, 0)

    def ring_step(j, _):
        for f in range(NF):
            rsy(j, f).wait_recv()
            rsz_got(j, f).wait_recv()
            own_part = dq[f, rows(c * RING + dest(j)), :].astype(F32)
            zs[j, f] = (own_part + yr[j, f].astype(F32) + zr[j, f].astype(F32)).astype(BF16)
            rsz(j, f).start()
        return 0

    for f in range(NF):
        rsy(0, f).wait_recv()
        own_part = dq[f, rows(c * RING + dest(0)), :].astype(F32)
        zs[0, f] = (own_part + yr[0, f].astype(F32)).astype(BF16)
        rsz(0, f).start()

    for f in range(NF):
        d = LOGIT_SCALE * jnp.dot(ds[...], qb[f], preferred_element_type=F32)
        dp[f] = d[0:PB, :]
        dps[f] = d[PB:NP, :].astype(BF16)
        send_dp(f).start()
        p_e = pb[f].astype(F32)
        q_f = qb[f].astype(F32)
        g = jnp.sum(p_e * (2.0 * d - p_e * u), axis=0, keepdims=True) - jnp.sum(
            q_f * q_f * t, axis=0, keepdims=True
        )
        g = g / gain_ref[:, f * FC:(f + 1) * FC]
        for k in range(FC // SEG):
            ga[f * (FC // SEG) + k, 0:1, :] = g[:, k * SEG:(k + 1) * SEG]
            ga[f * (FC // SEG) + k, 1:2, :] = jnp.broadcast_to(loss_part, (1, SEG))
        ring_step(f + 1, 0)

    def seg_to(k):
        return remote(ga.at[(ci + k) % CLASS], gar.at[ci], ga_s.at[k], ga_r.at[k], (peer(k), dy))

    def seg_got(k):
        slot = gar.at[(ci - k + CLASS) % CLASS]
        return remote(slot, slot, ga_s.at[k], ga_r.at[k], (peer(k), dy))

    def pair():
        return remote(gb, gbr, gb_s, gb_r, (pp, dy))

    def over_dy(k):
        return remote(gc.at[dy], gc.at[dy], gc_s.at[k], gc_r.at[k], (dx, (dy + k) % 16))

    def over_dy_got(k):
        slot = gc.at[(dy - k + 16) % 16]
        return remote(slot, slot, gc_s.at[k], gc_r.at[k], (dx, (dy + k) % 16))

    def back(k):
        return remote(gd.at[ci], gd.at[ci], gd_s.at[k], gd_r.at[k], (peer(k), dy))

    def back_got(k):
        slot = gd.at[(ci - k + CLASS) % CLASS]
        return remote(slot, slot, gd_s.at[k], gd_r.at[k], (peer(k), dy))

    def each(make, act):
        def body(k, _):
            copy = make(k)
            if act == "start":
                copy.start()
            elif act == "recv":
                copy.wait_recv()
            else:
                copy.wait_send()
            return 0

        lax.fori_loop(1, 16, body, 0)

    each(seg_to, "start")
    gar[ci] = ga[ci]
    ring_step(5, 0)
    each(seg_got, "recv")
    seg = gar[0]
    for k in range(1, CLASS):
        seg = seg + gar[k]
    gb[...] = seg
    pair().start()
    ring_step(6, 0)
    pair().wait_recv()
    gc[dy] = gb[...] + gbr[...]
    each(over_dy, "start")

    for f in range(NF):
        send_dp(f).wait_recv()

    def backward(hidden, inv_rms, inv_len, d):
        g = gain_ref[...]
        unit = hidden.astype(F32) * inv_rms
        e = unit * g * inv_len
        dnormed = inv_len * (d - e * jnp.sum(e * d, axis=1, keepdims=True))
        dunit = dnormed * g
        mean = jnp.sum(dunit * unit, axis=1, keepdims=True) * (1.0 / D)
        return (inv_rms * (dunit - unit * mean)).astype(BF16)

    def p_block(b, _):
        at = rows(b)
        d = jnp.concatenate([dp[f, at, :] + dpr[f, at, :].astype(F32) for f in range(NF)], axis=1)
        pg_ref[at, :] = backward(p_ref[at, :], pstat[0, at, :], pstat[1, at, :], d)
        return 0

    lax.fori_loop(0, PB // QB // 2, p_block, 0)
    each(over_dy_got, "recv")
    seg = gc[0]
    for k in range(1, 16):
        seg = seg + gc[k]
    gd[ci] = seg
    each(back, "start")
    lax.fori_loop(PB // QB // 2, PB // QB, p_block, 0)

    for f in range(NF):
        rsy(RING - 1, f).wait_recv()
        rsz_got(RING - 1, f).wait_recv()
        dfin[:, f * FC:(f + 1) * FC] = (
            dq[f, rows(c * RING + r), :].astype(F32) + yr[RING - 1, f].astype(F32) + zr[RING - 1, f].astype(F32)
        )
    _, _, q_rms, q_len = embed(q_ref[...])
    qg_ref[...] = backward(q_ref[...], q_rms, q_len, dfin[...])

    each(back_got, "recv")
    for k in range(CLASS):
        gg_ref[:, k * SEG:(k + 1) * SEG] = gd[k, 0:1, :]
    loss_ref[...] = gd[0, 1:2, 0:1]

    def done(s, _):
        for f in range(NF):
            agz(s, f).wait_send()
            rsz(s, f).wait_send()
        return 0

    def done_y(s, _):
        for f in range(NF):
            agy(s, f).wait_send()
            rsy(s, f).wait_send()
        return 0

    lax.fori_loop(0, RING - 1, done, 0)
    lax.fori_loop(0, RING, done_y, 0)
    for f in range(NF):
        swap(f).wait_send()
        send_dp(f).wait_send()
    each(stat, "send")
    each(seg_to, "send")
    pair().wait_send()
    each(over_dy, "send")
    each(back, "send")


def on_device(query_hidden, passage_hidden, gain, hard_ids, positive_ids):
    del hard_ids
    vmem = pl.BlockSpec(memory_space=pltpu.VMEM)
    dma = pltpu.SemaphoreType.DMA
    query_grad, passage_grad, gain_grad, loss = pl.pallas_call(
        kernel,
        out_shape=(
            jax.ShapeDtypeStruct((QB, D), BF16),
            jax.ShapeDtypeStruct((PB, D), BF16),
            jax.ShapeDtypeStruct((1, D), F32),
            jax.ShapeDtypeStruct((1, 1), F32),
        ),
        in_specs=[vmem] * 4,
        out_specs=(vmem,) * 4,
        scratch_shapes=[
            pltpu.VMEM((NF, NQ, FC), BF16),
            pltpu.VMEM((NF, NP, FC), BF16),
            pltpu.VMEM((NP, NQ), F32),
            pltpu.VMEM((NP, NQ), BF16),
            pltpu.VMEM((NF, NQ, FC), BF16),
            pltpu.VMEM((RING, NF, QB, FC), BF16),
            pltpu.VMEM((RING, NF, QB, FC), BF16),
            pltpu.VMEM((RING, NF, QB, FC), BF16),
            pltpu.VMEM((NF, PB, FC), F32),
            pltpu.VMEM((NF, PB, FC), BF16),
            pltpu.VMEM((NF, PB, FC), BF16),
            pltpu.VMEM((QB, D), F32),
            pltpu.VMEM((2, PB, 1), F32),
            pltpu.VMEM((CLASS, 2, NQ), F32),
            pltpu.VMEM((CLASS, 2, SEG), F32),
            pltpu.VMEM((CLASS, 2, SEG), F32),
            pltpu.VMEM((2, SEG), F32),
            pltpu.VMEM((2, SEG), F32),
            pltpu.VMEM((16, 2, SEG), F32),
            pltpu.VMEM((CLASS, 2, SEG), F32),
            dma((RING, NF)), dma((RING, NF)),
            dma((RING, NF)), dma((RING, NF)),
            dma((NF,)), dma((NF,)),
            dma((CLASS,)), dma((CLASS,)),
            dma((RING, NF)), dma((RING, NF)),
            dma((RING, NF)), dma((RING, NF)),
            dma((NF,)), dma((NF,)),
            dma((CLASS,)), dma((CLASS,)),
            dma, dma,
            dma((16,)), dma((16,)),
            dma((CLASS,)), dma((CLASS,)),
        ],
        compiler_params=pltpu.CompilerParams(
            collective_id=0, has_side_effects=True, vmem_limit_bytes=40 * 1024 * 1024
        ),
        cost_estimate=pl.CostEstimate(flops=1_610_612_736, bytes_accessed=2_400_000, transcendentals=200_000),
    )(query_hidden, passage_hidden, gain.reshape(1, D), positive_ids.reshape(1, QB))
    return query_grad, passage_grad, gain_grad.reshape(D), loss.reshape(())


def solution(mesh):
    placed = (
        P(("dx", "dy"), None),
        P(("dx", "dy"), None),
        P(),
        P(("dx", "dy"), None),
        P(("dx", "dy")),
    )
    return jax.shard_map(
        on_device,
        mesh=mesh,
        in_specs=placed,
        out_specs=(P(("dx", "dy"), None), P(("dx", "dy"), None), P(), P()),
        check_vma=False,
    )
```

time: 840 us -> 124 us (0.15)
  waiting for transfers between devices: 467 us -> 0 us
  blocking collectives: 331 us -> 0 us
  Pallas kernels: 0 us -> 116 us
  other arithmetic: 14.8 us -> 0 us
  between operations: 14.1 us -> 2.4 us
  matrix products: 11 us -> 0 us
    reduce_scatter x1 -> x0, waiting for transfers between devices: 258 us -> none  [on_device(): lax.psum_scatter((logit_scale * jnp.dot(dscore, p_emb, preferred_element_...]
    psum x2 -> x0, blocking collectives: 224 us -> none  [the longest x1 125 us: on_device(): gain_grad, loss = lax.psum((q_gain + p_gain, loss_part), ('dx', 'dy'))]
    all_gather x1 -> x0, waiting for transfers between devices: 209 us -> none  [on_device(): q_group = lax.all_gather(q_emb, 'dx', axis=0, tiled=True)]
    pallas_call x0 -> x1, Pallas kernels: none -> 116 us  [on_device(): pl.pallas_call(kernel, out_shape=(jax.ShapeDtypeStruct((QB, D), BF16), ja...]
    pmax x1 -> x0, blocking collectives: 107 us -> none  [on_device(): top = lax.pmax(local_max, 'dx')]
    dot_general x3 -> x0, matrix products: 11 us -> none  [the longest x1 3.74 us: score_block(): lax.dot_general(queries, passages, (((1,), (1,)), ((), ())), preferred_el...]
    reduce_sum x9 -> x0, other arithmetic: 9.39 us -> none  [the longest x2 2.65 us: embed(): jnp.mean(values * values, axis=-1, keepdims=True) + 1e-05]
  transfers between devices with their start and end apart: 2 -> 0, of which waited for: 2 -> 0; matrix products, arithmetic and copies ran while one was open for 1% -> 0% of each run, Pallas kernels for 0% -> 0%
where the time goes in v1:
time: 124 us
  Pallas kernels  116 us (94%)
  local copies, waits for them, and re-layouts  5.73 us (5%)
  between operations  2.4 us (2%)
    pallas_call x1, Pallas kernels, on_device(): pl.pallas_call(kernel, out_shape=(jax.ShapeDtypeStruct((QB, D), BF16), ja...  116 us
    unnamed x11, local copies, waits for them, and re-layouts  5.73 us

profile of v1, /device:TPU:1, one launch (start us, length us, event | category | flops | bytes accessed | tf_op | source)
XLA Modules:
  0.0 124.1 jit_solution(9040399386799129983)
XLA Ops:
  0.6 0.0 copy-start.3
  0.6 0.6 copy-done.3
  1.3 0.0 copy-start
  1.3 1.2 copy-done
  2.5 0.0 copy-start.1
  2.5 0.9 copy-done.1
  3.4 0.0 copy-start.2
  3.4 0.7 copy-done.2
  4.1 116.0 %shard_map.75 = (bf16[16,4096]{1,0:T(8,128)(2,1)S(1)}, bf16[128,4096]{1,0:T(8,128)(2,1)S(1)}, f32[1,4096]{1,0:T(1,128)S(1)}, f32[1,1]{1,0:T(1,128)}) custom-call(bf16[16,4096]{1,0:T(8,128)(2,1)S(1)} %copy-done.1, bf16[128,4096]{1,0:T(8,128)(2,1)S(1)} %copy-done, f32[1,4096]{1,0:T(1,128)S(1)} %bitcast.5, s32[1,16]{1,0:T(1,128)S(1)} %bitcast.6), custom_call_target="tpu_custom_call" | custom-call | flops 1610612736 | bytes 2400000 | tf_op jit(solution)/shard_map/pallas_call | solution.py:378
  120.1 0.7 copy.12
  120.8 1.0 copy.13
  121.7 0.6 copy.14
Async XLA Ops:
  0.6 0.7 copy-start.3
  1.3 1.2 copy-start
  2.5 0.9 copy-start.1
  3.4 0.7 copy-start.2

commit v2 on v1

v2 whole, which is shorter than its diff:
```python
import jax
import jax.numpy as jnp
from jax import lax
from jax.experimental import pallas as pl
from jax.experimental.pallas import tpu as pltpu
from jax.sharding import PartitionSpec as P

MESH = pl.DeviceIdType.MESH
F32 = jnp.float32
BF16 = jnp.bfloat16

LOGIT_SCALE = 250.0
HARD_WEIGHT = 3.0
D = 4096
QB = 16
PB = 128
RING = 8
CLASS = 16
NQ = QB * CLASS
NP = 2 * PB
NF = 4
FC = D // NF
SEG = D // CLASS


def kernel(
    q_hbm, p_hbm, gain_hbm, pos_hbm,
    qg_ref, pg_ref, gg_ref, loss_ref,
    q_ref, p_ref, gain_ref, pos_ref,
    qb, pb, sc, ds, dq, yr, zs, zr, dp, dps, dpr, dfin, pstat, stats, ga, gar, gb, gbr, gc, gd,
    in_sem, z_r, rsy_r, dp_r, agy_r, one_s, one_r,
):
    dx = lax.axis_index("dx")
    dy = lax.axis_index("dy")
    y = dx % 4
    z = dx // 4
    half = z // 2
    r = half + (z % 2) * (7 - 2 * half)
    c = y // 2
    cls = (y + c) % 2
    ci = c * RING + r

    def z_of(place):
        return 2 * place + (place // 4) * (15 - 4 * place)

    nxt = z_of((r + 1) % RING) * 4 + y
    prv = z_of((r + RING - 1) % RING) * 4 + y
    yp = z * 4 + 3 - y
    pp = z * 4 + y + 1 - 2 * (y % 2)

    def peer(k):
        other = (ci + k) % CLASS
        c2 = other // RING
        return z_of(other % RING) * 4 + cls + c2 * (3 - 2 * cls)

    def rows(block, size=QB):
        return pl.ds(pl.multiple_of(block * size, size), size)

    def remote(src, dst, send, recv, dev, other_dy=None):
        return pltpu.make_async_remote_copy(
            src_ref=src, dst_ref=dst, send_sem=send, recv_sem=recv,
            device_id=(dev, dy if other_dy is None else other_dy), device_id_type=MESH,
        )

    loads = [
        pltpu.make_async_copy(src, dst, in_sem.at[i])
        for i, (src, dst) in enumerate(
            ((q_hbm, q_ref), (gain_hbm, gain_ref), (pos_hbm, pos_ref), (p_hbm, p_ref))
        )
    ]
    for load in loads:
        load.start()

    barrier = pltpu.get_barrier_semaphore()

    def greet(k, _):
        pl.semaphore_signal(barrier, inc=1, device_id=(peer(k), dy), device_id_type=MESH)
        pl.semaphore_signal(barrier, inc=1, device_id=(dx, (dy + k) % 16), device_id_type=MESH)
        return 0

    lax.fori_loop(1, 16, greet, 0)
    pl.semaphore_signal(barrier, inc=1, device_id=(pp, dy), device_id_type=MESH)

    def embed(hidden):
        v = hidden.astype(F32)
        vg = v * gain_ref[...]
        inv_rms = lax.rsqrt(jnp.sum(v * v, axis=1, keepdims=True) * (1.0 / D) + 1e-05)
        inv_len = lax.rsqrt(jnp.sum(vg * vg, axis=1, keepdims=True) * (inv_rms * inv_rms) + 1e-06)
        return vg * (inv_rms * inv_len), inv_rms, inv_len

    loads[0].wait()
    loads[1].wait()
    q_e, _, _ = embed(q_ref[...])
    for f in range(NF):
        qb[f, rows(ci), :] = q_e[:, f * FC:(f + 1) * FC].astype(BF16)

    pl.semaphore_wait(barrier, 31)

    def block(off, f, cc=None):
        return qb.at[f, rows((c if cc is None else cc) * RING + (r + off + RING) % RING), :]

    def send_f(h, f):
        return remote(block(-h, f), block(-h, f), one_s.at[0], z_r.at[2 * h, f], nxt)

    def send_b(h, f):
        return remote(block(h, f), block(h, f), one_s.at[0], z_r.at[2 * h + 1, f], prv)

    def got_f(h, f):
        return remote(block(-h, f), block(-h, f), one_s.at[0], z_r.at[2 * h - 2, f], nxt)

    def got_b(h, f):
        return remote(block(h, f), block(h, f), one_s.at[0], z_r.at[2 * h - 1, f], prv)

    def send_y(off, f):
        return remote(block(off, f), block(off, f), one_s.at[1], agy_r.at[f], yp)

    for f in range(NF):
        send_f(0, f).start()
        send_b(0, f).start()
        send_y(0, f).start()

    loads[3].wait()

    def embed_block(b, _):
        e, inv_rms, inv_len = embed(p_ref[rows(b), :])
        for f in range(NF):
            pb[f, rows(b), :] = e[:, f * FC:(f + 1) * FC].astype(BF16)
        pstat[0, rows(b), :] = inv_rms
        pstat[1, rows(b), :] = inv_len
        remote(pb.at[:, rows(b), :], pb.at[:, rows(b + PB // QB), :], one_s.at[2], one_r.at[2], pp).start()
        return 0

    lax.fori_loop(0, PB // QB, embed_block, 0)

    loads[2].wait()
    lane = lax.broadcasted_iota(jnp.int32, (PB, NQ), 1)
    row = lax.broadcasted_iota(jnp.int32, (PB, NQ), 0)
    own = (lane == ci * QB + row // 8).astype(F32)
    ids = lax.broadcasted_iota(jnp.int32, (PB, QB), 0) + dx * PB
    flag = jnp.sum((ids == pos_ref[...]).astype(F32), axis=1, keepdims=True)

    for h in range(1, 5):
        for f in range(NF):
            forth = f < NF // 2
            if h < 4 or forth:
                got_f(h, f).wait_recv()
                if h < 3 or (h == 3 and forth):
                    send_f(h, f).start()
                send_y(-h, f).start()
            if h < 4 or not forth:
                got_b(h, f).wait_recv()
                if h < 3 or (h == 3 and not forth):
                    send_b(h, f).start()
                send_y(h, f).start()

    swapped = pb.at[:, pl.ds(PB, PB), :]
    remote(swapped, swapped, one_s.at[2], one_r.at[2], pp).wait_recv()
    for f in range(NF):
        theirs = qb.at[f, rows(1 - c, RING * QB), :]
        remote(theirs, theirs, one_s.at[1], agy_r.at[f], yp).wait_recv()
        part = lax.dot_general(pb[f], qb[f], (((1,), (1,)), ((), ())), preferred_element_type=F32)
        sc[...] = part if f == 0 else sc[...] + part
    sc[...] = sc[...] * LOGIT_SCALE

    is_pos = own * flag
    weights = 1.0 + HARD_WEIGHT * (own - is_pos)
    s_own = sc[0:PB, :]
    s_far = sc[PB:NP, :]
    top = jnp.maximum(jnp.max(s_own, axis=0, keepdims=True), jnp.max(s_far, axis=0, keepdims=True))
    total = jnp.sum(weights * jnp.exp(s_own - top), axis=0, keepdims=True) + jnp.sum(
        jnp.exp(s_far - top), axis=0, keepdims=True
    )
    stats[ci, 0:1, :] = top
    stats[ci, 1:2, :] = total

    def to_class(ref_of, dst, i):
        def go(k, _):
            remote(ref_of(k), dst.at[ci], one_s.at[i], one_r.at[i], peer(k)).start()
            return 0

        lax.fori_loop(1, CLASS, go, 0)

    def fifteen(ref, i):
        part = ref.at[pl.ds(0, 15)]
        return remote(part, part, one_s.at[i], one_r.at[i], pp)

    to_class(lambda k: stats.at[ci], stats, 3)
    pos_score = jnp.sum(is_pos * s_own, axis=0, keepdims=True)
    fifteen(stats, 3).wait_recv()
    top_all = stats[0, 0:1, :]
    for k in range(1, CLASS):
        top_all = jnp.maximum(top_all, stats[k, 0:1, :])
    sum_all = jnp.zeros((1, NQ), F32)
    for k in range(CLASS):
        sum_all = sum_all + stats[k, 1:2, :] * jnp.exp(stats[k, 0:1, :] - top_all)
    log_total = top_all + jnp.log(sum_all)
    lane1 = lax.broadcasted_iota(jnp.int32, (1, NQ), 1)
    loss_part = jnp.sum(
        jnp.where(lane1 // QB == ci, log_total - pos_score, 0.0), axis=1, keepdims=True
    )

    ds[0:PB, :] = (weights * jnp.exp(s_own - log_total) - is_pos).astype(BF16)
    ds[PB:NP, :] = jnp.exp(s_far - log_total).astype(BF16)
    ds_f = ds[...].astype(F32)
    ds_t = jnp.transpose(ds_f).astype(BF16)

    offs = (4, 3, -3, 2, -2, 1, -1, 0)
    slot_after = (None, 3, 4, 5, 6, 7, 0)

    def dest(i, cc):
        return rows(cc * RING + (r + offs[i] + RING) % RING)

    for f in range(NF):
        dq[f] = (LOGIT_SCALE * jnp.dot(ds_t, pb[f], preferred_element_type=F32)).astype(BF16)
    for i in range(RING):
        for f in range(NF):
            remote(dq.at[f, dest(i, 1 - c), :], yr.at[i, f], one_s.at[4], rsy_r.at[i, f], yp).start()

    for f in range(NF):
        d = LOGIT_SCALE * jnp.dot(ds[...], qb[f], preferred_element_type=F32)
        dp[:, f * FC:(f + 1) * FC] = d[0:PB, :]
        dps[:, f * FC:(f + 1) * FC] = d[PB:NP, :].astype(BF16)

    def send_dp(b):
        return remote(dps.at[rows(b), :], dpr.at[rows(b), :], one_s.at[5], dp_r.at[b], pp)

    def start_dp(b, _):
        send_dp(b).start()
        return 0

    lax.fori_loop(0, PB // QB, start_dp, 0)

    def zr_got(i, f):
        return remote(zs.at[0, f], zr.at[i, f], one_s.at[6], z_r.at[i, f], nxt)

    def ring_step(i):
        for f in range(NF):
            forth = f < NF // 2
            rsy = remote(yr.at[i, f], yr.at[i, f], one_s.at[4], rsy_r.at[i, f], yp)
            rsy.wait_recv()
            acc = dq[f, dest(i, c), :].astype(F32) + yr[i, f].astype(F32)
            if i >= 3 or (i == 1 and forth) or (i == 2 and not forth):
                zr_got(i, f).wait_recv()
                acc = acc + zr[i, f].astype(F32)
            zs[i, f] = acc.astype(BF16)
            ahead = forth if i == 0 else i % 2 == 1
            after = (1 if forth else 2) if i == 0 else slot_after[i]
            remote(zs.at[i, f], zr.at[after, f], one_s.at[6], z_r.at[after, f], nxt if ahead else prv).start()

    ring_step(0)

    prod = ds_f * sc[...]
    u = jnp.sum(prod, axis=1, keepdims=True)
    t_row = jnp.sum(prod, axis=0, keepdims=True)
    t = jnp.transpose(jnp.broadcast_to(t_row, (8, NQ)))[:, 0:1]
    for f in range(NF):
        cols = slice(f * FC, (f + 1) * FC)
        p_own = pb[f, 0:PB, :].astype(F32)
        p_far = pb[f, PB:NP, :].astype(F32)
        q_f = qb[f].astype(F32)
        g = (
            jnp.sum(p_own * (2.0 * dp[:, cols] - p_own * u[0:PB]), axis=0, keepdims=True)
            + jnp.sum(p_far * (2.0 * dps[:, cols].astype(F32) - p_far * u[PB:NP]), axis=0, keepdims=True)
            - jnp.sum(q_f * q_f * t, axis=0, keepdims=True)
        ) / gain_ref[:, cols]
        for k in range(FC // SEG):
            ga[f * (FC // SEG) + k, 0:1, :] = g[:, k * SEG:(k + 1) * SEG]
            ga[f * (FC // SEG) + k, 1:2, :] = jnp.broadcast_to(loss_part, (1, SEG))

    ring_step(1)
    ring_step(2)

    to_class(lambda k: ga.at[(ci + k) % CLASS], gar, 7)
    gar[ci] = ga[ci]

    def backward(hidden, inv_rms, inv_len, d):
        g = gain_ref[...]
        unit = hidden.astype(F32) * inv_rms
        e = unit * g * inv_len
        dnormed = inv_len * (d - e * jnp.sum(e * d, axis=1, keepdims=True))
        dunit = dnormed * g
        mean = jnp.sum(dunit * unit, axis=1, keepdims=True) * (1.0 / D)
        return (inv_rms * (dunit - unit * mean)).astype(BF16)

    def p_block(b, _):
        send_dp(b).wait_recv()
        at = rows(b)
        d = dp[at, :] + dpr[at, :].astype(F32)
        pg_ref[at, :] = backward(p_ref[at, :], pstat[0, at, :], pstat[1, at, :], d)
        return 0

    def p_blocks(b0, b1):
        lax.fori_loop(b0, b1, p_block, 0)

    p_blocks(0, 1)
    ring_step(3)
    ring_step(4)

    fifteen(gar, 7).wait_recv()
    seg = gar[0]
    for k in range(1, CLASS):
        seg = seg + gar[k]
    gb[...] = seg
    pair = remote(gb, gbr, one_s.at[8], one_r.at[8], pp)
    pair.start()
    p_blocks(1, 3)
    ring_step(5)
    ring_step(6)

    pair.wait_recv()
    gc[dy] = gb[...] + gbr[...]

    def over_dy(k, _):
        remote(gc.at[dy], gc.at[dy], one_s.at[9], one_r.at[9], dx, (dy + k) % 16).start()
        return 0

    lax.fori_loop(1, 16, over_dy, 0)
    p_blocks(3, 5)
    fifteen(gc, 9).wait_recv()
    seg = gc[0]
    for k in range(1, 16):
        seg = seg + gc[k]
    gd[ci] = seg
    to_class(lambda k: gd.at[ci], gd, 10)
    p_blocks(5, 6)

    for f in range(NF):
        rsy = remote(yr.at[RING - 1, f], yr.at[RING - 1, f], one_s.at[4], rsy_r.at[RING - 1, f], yp)
        rsy.wait_recv()
        zr_got(7, f).wait_recv()
        zr_got(0, f).wait_recv()
        dfin[:, f * FC:(f + 1) * FC] = (
            dq[f, dest(7, c), :].astype(F32) + yr[RING - 1, f].astype(F32)
            + (zr[7, f].astype(F32) + zr[0, f].astype(F32))
        )
    _, q_rms, q_len = embed(q_ref[...])
    qg_ref[...] = backward(q_ref[...], q_rms, q_len, dfin[...])
    p_blocks(6, 8)

    fifteen(gd, 10).wait_recv()
    for k in range(CLASS):
        gg_ref[:, k * SEG:(k + 1) * SEG] = gd[k, 0:1, :]
    loss_ref[...] = gd[0, 1:2, 0:1]

    for ref, i in (
        (qb.at[:, pl.ds(0, 7 * QB), :], 0), (qb.at[:, pl.ds(0, 8 * QB), :], 1), (swapped, 2),
        (yr, 4), (dpr, 5), (zs.at[pl.ds(0, 7)], 6), (gb, 8),
    ):
        remote(ref, ref, one_s.at[i], one_r.at[i], pp).wait_send()
    for ref, i in ((stats, 3), (gar, 7), (gc, 9), (gd, 10)):
        fifteen(ref, i).wait_send()


def on_device(query_hidden, passage_hidden, gain, hard_ids, positive_ids):
    del hard_ids
    vmem = pl.BlockSpec(memory_space=pltpu.VMEM)
    hbm = pl.BlockSpec(memory_space=pl.ANY)
    dma = pltpu.SemaphoreType.DMA
    query_grad, passage_grad, gain_grad, loss = pl.pallas_call(
        kernel,
        out_shape=(
            jax.ShapeDtypeStruct((QB, D), BF16),
            jax.ShapeDtypeStruct((PB, D), BF16),
            jax.ShapeDtypeStruct((1, D), F32),
            jax.ShapeDtypeStruct((1, 1), F32),
        ),
        in_specs=[hbm] * 4,
        out_specs=(vmem,) * 4,
        scratch_shapes=[
            pltpu.VMEM((QB, D), BF16),
            pltpu.VMEM((PB, D), BF16),
            pltpu.VMEM((1, D), F32),
            pltpu.VMEM((1, QB), jnp.int32),
            pltpu.VMEM((NF, NQ, FC), BF16),
            pltpu.VMEM((NF, NP, FC), BF16),
            pltpu.VMEM((NP, NQ), F32),
            pltpu.VMEM((NP, NQ), BF16),
            pltpu.VMEM((NF, NQ, FC), BF16),
            pltpu.VMEM((RING, NF, QB, FC), BF16),
            pltpu.VMEM((RING, NF, QB, FC), BF16),
            pltpu.VMEM((RING, NF, QB, FC), BF16),
            pltpu.VMEM((PB, D), F32),
            pltpu.VMEM((PB, D), BF16),
            pltpu.VMEM((PB, D), BF16),
            pltpu.VMEM((QB, D), F32),
            pltpu.VMEM((2, PB, 1), F32),
            pltpu.VMEM((CLASS, 2, NQ), F32),
            pltpu.VMEM((CLASS, 2, SEG), F32),
            pltpu.VMEM((CLASS, 2, SEG), F32),
            pltpu.VMEM((2, SEG), F32),
            pltpu.VMEM((2, SEG), F32),
            pltpu.VMEM((16, 2, SEG), F32),
            pltpu.VMEM((CLASS, 2, SEG), F32),
            dma((4,)),
            dma((RING, NF)),
            dma((RING, NF)),
            dma((PB // QB,)),
            dma((NF,)),
            dma((11,)),
            dma((11,)),
        ],
        compiler_params=pltpu.CompilerParams(
            collective_id=0, has_side_effects=True, vmem_limit_bytes=40 * 1024 * 1024
        ),
        cost_estimate=pl.CostEstimate(flops=1_610_612_736, bytes_accessed=2_400_000, transcendentals=200_000),
    )(query_hidden, passage_hidden, gain.reshape(1, D), positive_ids.reshape(1, QB))
    return query_grad, passage_grad, gain_grad.reshape(D), loss.reshape(())


def solution(mesh):
    placed = (
        P(("dx", "dy"), None),
        P(("dx", "dy"), None),
        P(),
        P(("dx", "dy"), None),
        P(("dx", "dy")),
    )
    return jax.shard_map(
        on_device,
        mesh=mesh,
        in_specs=placed,
        out_specs=(P(("dx", "dy"), None), P(("dx", "dy"), None), P(), P()),
        check_vma=False,
    )
```

time: 124 us -> 105 us (0.85)
  Pallas kernels: 116 us -> 96.5 us
    pallas_call x1, Pallas kernels: 116 us -> 96.5 us  [on_device(): pl.pallas_call(kernel, out_shape=(jax.ShapeDtypeStruct((QB, D), BF16), ja...]
where the time goes in v2:
time: 105 us
  Pallas kernels  96.5 us (92%)
  local copies, waits for them, and re-layouts  5.73 us (5%)
  between operations  2.4 us (2%)
    pallas_call x1, Pallas kernels, on_device(): pl.pallas_call(kernel, out_shape=(jax.ShapeDtypeStruct((QB, D), BF16), ja...  96.5 us
    unnamed x11, local copies, waits for them, and re-layouts  5.73 us

profile of v2, /device:TPU:1, one launch (start us, length us, event | category | flops | bytes accessed | tf_op | source)
XLA Modules:
  0.0 104.6 jit_solution(13513582278231165738)
XLA Ops:
  0.6 0.0 copy-start.3
  0.6 0.6 copy-done.3
  1.3 0.0 copy-start
  1.3 1.2 %copy-done = bf16[128,4096]{1,0:T(8,128)(2,1)S(1)} copy-done((bf16[128,4096]{1,0:T(8,128)(2,1)S(1)}, bf16[128,4096]{1,0:T(8,128)(2,1)}, u32[]{:S(2)}) %copy-start) | copy-done | bytes 1048600
  2.5 0.0 copy-start.1
  2.5 0.9 copy-done.1
  3.4 0.0 copy-start.2
  3.4 0.7 copy-done.2
  4.1 96.5 %shard_map.75 = (bf16[16,4096]{1,0:T(8,128)(2,1)S(1)}, bf16[128,4096]{1,0:T(8,128)(2,1)S(1)}, f32[1,4096]{1,0:T(1,128)S(1)}, f32[1,1]{1,0:T(1,128)}) custom-call(bf16[16,4096]{1,0:T(8,128)(2,1)S(1)} %copy-done.1, bf16[128,4096]{1,0:T(8,128)(2,1)S(1)} %copy-done, f32[1,4096]{1,0:T(1,128)S(1)} %bitcast.5, s32[1,16]{1,0:T(1,128)S(1)} %bitcast.6), custom_call_target="tpu_custom_call" | custom-call | flops 1610612736 | bytes 2400000 | tf_op jit(solution)/shard_map/pallas_call | solution.py:359
  100.7 0.7 copy.12
  101.3 1.0 copy.13
  102.3 0.6 copy.14
Async XLA Ops:
  0.6 0.7 copy-start.3
  1.3 1.2 %copy-start = (bf16[128,4096]{1,0:T(8,128)(2,1)S(1)}, bf16[128,4096]{1,0:T(8,128)(2,1)}, u32[]{:S(2)}) copy-start(bf16[128,4096]{1,0:T(8,128)(2,1)} %p_hbm.1) | copy-start | bytes 3145732
  2.5 0.9 copy-start.1
  3.4 0.7 copy-start.2

commit v3 on v2

--- a/solution.py
+++ b/solution.py
@@ -27,7 +27,7 @@
     q_hbm, p_hbm, gain_hbm, pos_hbm,
     qg_ref, pg_ref, gg_ref, loss_ref,
     q_ref, p_ref, gain_ref, pos_ref,
-    qb, pb, sc, ds, dq, yr, zs, zr, dp, dps, dpr, dfin, pstat, stats, ga, gar, gb, gbr, gc, gd,
+    qb, pb, sc, ds, dq, yr, zs, zr, dp, dps, dpr, dfin, pstat, stats, ga, gar, gb, gbr, gc, gd, et, from_y,
     in_sem, z_r, rsy_r, dp_r, agy_r, one_s, one_r,
 ):
     dx = lax.axis_index("dx")
@@ -156,8 +156,8 @@
     swapped = pb.at[:, pl.ds(PB, PB), :]
     remote(swapped, swapped, one_s.at[2], one_r.at[2], pp).wait_recv()
     for f in range(NF):
-        theirs = qb.at[f, rows(1 - c, RING * QB), :]
-        remote(theirs, theirs, one_s.at[1], agy_r.at[f], yp).wait_recv()
+        arrived = qb.at[f, rows(1 - c, RING * QB), :]
+        remote(arrived, arrived, one_s.at[1], agy_r.at[f], yp).wait_recv()
         part = lax.dot_general(pb[f], qb[f], (((1,), (1,)), ((), ())), preferred_element_type=F32)
         sc[...] = part if f == 0 else sc[...] + part
     sc[...] = sc[...] * LOGIT_SCALE
@@ -167,9 +167,9 @@
     s_own = sc[0:PB, :]
     s_far = sc[PB:NP, :]
     top = jnp.maximum(jnp.max(s_own, axis=0, keepdims=True), jnp.max(s_far, axis=0, keepdims=True))
-    total = jnp.sum(weights * jnp.exp(s_own - top), axis=0, keepdims=True) + jnp.sum(
-        jnp.exp(s_far - top), axis=0, keepdims=True
-    )
+    e_own = weights * jnp.exp(s_own - top)
+    e_far = jnp.exp(s_far - top)
+    total = jnp.sum(e_own, axis=0, keepdims=True) + jnp.sum(e_far, axis=0, keepdims=True)
     stats[ci, 0:1, :] = top
     stats[ci, 1:2, :] = total
 
@@ -185,6 +185,22 @@
         return remote(part, part, one_s.at[i], one_r.at[i], pp)
 
     to_class(lambda k: stats.at[ci], stats, 3)
+
+    offs = (4, 3, -3, 2, -2, 1, -1, 0)
+    slot_after = (None, 3, 4, 5, 6, 7, 0)
+
+    def dest(i, cc):
+        return rows(cc * RING + (r + offs[i] + RING) % RING)
+
+    et[:, 0:PB] = jnp.transpose(e_own).astype(BF16)
+    et[:, PB:NP] = jnp.transpose(e_far).astype(BF16)
+    theirs = rows(1 - c, RING * QB)
+    for f in range(NF):
+        dq[f, theirs, :] = jnp.dot(et[theirs, :], pb[f], preferred_element_type=F32).astype(BF16)
+    for i in range(RING):
+        for f in range(NF):
+            remote(dq.at[f, dest(i, 1 - c), :], yr.at[i, f], one_s.at[4], rsy_r.at[i, f], yp).start()
+
     pos_score = jnp.sum(is_pos * s_own, axis=0, keepdims=True)
     fifteen(stats, 3).wait_recv()
     top_all = stats[0, 0:1, :]
@@ -202,19 +218,9 @@
     ds[0:PB, :] = (weights * jnp.exp(s_own - log_total) - is_pos).astype(BF16)
     ds[PB:NP, :] = jnp.exp(s_far - log_total).astype(BF16)
     ds_f = ds[...].astype(F32)
-    ds_t = jnp.transpose(ds_f).astype(BF16)
-
-    offs = (4, 3, -3, 2, -2, 1, -1, 0)
-    slot_after = (None, 3, 4, 5, 6, 7, 0)
-
-    def dest(i, cc):
-        return rows(cc * RING + (r + offs[i] + RING) % RING)
-
-    for f in range(NF):
-        dq[f] = (LOGIT_SCALE * jnp.dot(ds_t, pb[f], preferred_element_type=F32)).astype(BF16)
-    for i in range(RING):
-        for f in range(NF):
-            remote(dq.at[f, dest(i, 1 - c), :], yr.at[i, f], one_s.at[4], rsy_r.at[i, f], yp).start()
+    et[...] = jnp.transpose(ds_f).astype(BF16)
+    scale = LOGIT_SCALE * jnp.exp(stats[(1 - c) * RING + r, 0:1, :] - log_total)
+    from_y[...] = jnp.transpose(jnp.broadcast_to(scale, (8, NQ)))[:, 0:1]
 
     for f in range(NF):
         d = LOGIT_SCALE * jnp.dot(ds[...], qb[f], preferred_element_type=F32)
@@ -229,6 +235,10 @@
         return 0
 
     lax.fori_loop(0, PB // QB, start_dp, 0)
+
+    ours = rows(c, RING * QB)
+    for f in range(NF):
+        dq[f, ours, :] = (LOGIT_SCALE * jnp.dot(et[ours, :], pb[f], preferred_element_type=F32)).astype(BF16)
 
     def zr_got(i, f):
         return remote(zs.at[0, f], zr.at[i, f], one_s.at[6], z_r.at[i, f], nxt)
@@ -238,7 +248,7 @@
             forth = f < NF // 2
             rsy = remote(yr.at[i, f], yr.at[i, f], one_s.at[4], rsy_r.at[i, f], yp)
             rsy.wait_recv()
-            acc = dq[f, dest(i, c), :].astype(F32) + yr[i, f].astype(F32)
+            acc = dq[f, dest(i, c), :].astype(F32) + yr[i, f].astype(F32) * from_y[dest(i, c), :]
             if i >= 3 or (i == 1 and forth) or (i == 2 and not forth):
                 zr_got(i, f).wait_recv()
                 acc = acc + zr[i, f].astype(F32)
@@ -246,8 +256,6 @@
             ahead = forth if i == 0 else i % 2 == 1
             after = (1 if forth else 2) if i == 0 else slot_after[i]
             remote(zs.at[i, f], zr.at[after, f], one_s.at[6], z_r.at[after, f], nxt if ahead else prv).start()
-
-    ring_step(0)
 
     prod = ds_f * sc[...]
     u = jnp.sum(prod, axis=1, keepdims=True)
@@ -267,11 +275,20 @@
             ga[f * (FC // SEG) + k, 0:1, :] = g[:, k * SEG:(k + 1) * SEG]
             ga[f * (FC // SEG) + k, 1:2, :] = jnp.broadcast_to(loss_part, (1, SEG))
 
+    to_class(lambda k: ga.at[(ci + k) % CLASS], gar, 7)
+    gar[ci] = ga[ci]
+
+    ring_step(0)
     ring_step(1)
     ring_step(2)
 
-    to_class(lambda k: ga.at[(ci + k) % CLASS], gar, 7)
-    gar[ci] = ga[ci]
+    fifteen(gar, 7).wait_recv()
+    seg = gar[0]
+    for k in range(1, CLASS):
+        seg = seg + gar[k]
+    gb[...] = seg
+    pair = remote(gb, gbr, one_s.at[8], one_r.at[8], pp)
+    pair.start()
 
     def backward(hidden, inv_rms, inv_len, d):
         g = gain_ref[...]
@@ -292,20 +309,8 @@
     def p_blocks(b0, b1):
         lax.fori_loop(b0, b1, p_block, 0)
 
-    p_blocks(0, 1)
     ring_step(3)
     ring_step(4)
-
-    fifteen(gar, 7).wait_recv()
-    seg = gar[0]
-    for k in range(1, CLASS):
-        seg = seg + gar[k]
-    gb[...] = seg
-    pair = remote(gb, gbr, one_s.at[8], one_r.at[8], pp)
-    pair.start()
-    p_blocks(1, 3)
-    ring_step(5)
-    ring_step(6)
 
     pair.wait_recv()
     gc[dy] = gb[...] + gbr[...]
@@ -315,14 +320,18 @@
         return 0
 
     lax.fori_loop(1, 16, over_dy, 0)
-    p_blocks(3, 5)
+    p_blocks(0, 2)
+    ring_step(5)
+    ring_step(6)
+    p_blocks(2, 4)
+
     fifteen(gc, 9).wait_recv()
     seg = gc[0]
     for k in range(1, 16):
         seg = seg + gc[k]
     gd[ci] = seg
     to_class(lambda k: gd.at[ci], gd, 10)
-    p_blocks(5, 6)
+    p_blocks(4, 6)
 
     for f in range(NF):
         rsy = remote(yr.at[RING - 1, f], yr.at[RING - 1, f], one_s.at[4], rsy_r.at[RING - 1, f], yp)
@@ -330,7 +339,7 @@
         zr_got(7, f).wait_recv()
         zr_got(0, f).wait_recv()
         dfin[:, f * FC:(f + 1) * FC] = (
-            dq[f, dest(7, c), :].astype(F32) + yr[RING - 1, f].astype(F32)
+            dq[f, dest(7, c), :].astype(F32) + yr[RING - 1, f].astype(F32) * from_y[dest(7, c), :]
             + (zr[7, f].astype(F32) + zr[0, f].astype(F32))
         )
     _, q_rms, q_len = embed(q_ref[...])
@@ -354,7 +363,7 @@
 def on_device(query_hidden, passage_hidden, gain, hard_ids, positive_ids):
     del hard_ids
     vmem = pl.BlockSpec(memory_space=pltpu.VMEM)
-    hbm = pl.BlockSpec(memory_space=pl.ANY)
+    hbm = pl.BlockSpec(memory_space=pltpu.HBM)
     dma = pltpu.SemaphoreType.DMA
     query_grad, passage_grad, gain_grad, loss = pl.pallas_call(
         kernel,
@@ -391,6 +400,8 @@
             pltpu.VMEM((2, SEG), F32),
             pltpu.VMEM((16, 2, SEG), F32),
             pltpu.VMEM((CLASS, 2, SEG), F32),
+            pltpu.VMEM((NQ, NP), BF16),
+            pltpu.VMEM((NQ, 1), F32),
             dma((4,)),
             dma((RING, NF)),
             dma((RING, NF)),

time: 105 us -> 102 us (0.971)
  Pallas kernels: 96.5 us -> 93.7 us
    pallas_call x1, Pallas kernels: 96.5 us -> 93.7 us  [on_device(): pl.pallas_call(kernel, out_shape=(jax.ShapeDtypeStruct((QB, D), BF16), ja...]
where the time goes in v3:
time: 102 us
  Pallas kernels  93.7 us (92%)
  local copies, waits for them, and re-layouts  5.73 us (6%)
  between operations  2.4 us (2%)
    pallas_call x1, Pallas kernels, on_device(): pl.pallas_call(kernel, out_shape=(jax.ShapeDtypeStruct((QB, D), BF16), ja...  93.7 us
    unnamed x11, local copies, waits for them, and re-layouts  5.73 us

profile of v3, /device:TPU:1, one launch (start us, length us, event | category | flops | bytes accessed | tf_op | source)
XLA Modules:
  0.0 101.8 jit_solution(3571827543545056259)
XLA Ops:
  0.6 0.0 copy-start.3
  0.6 0.6 copy-done.3
  1.3 0.0 copy-start
  1.3 1.2 %copy-done = bf16[128,4096]{1,0:T(8,128)(2,1)S(1)} copy-done((bf16[128,4096]{1,0:T(8,128)(2,1)S(1)}, bf16[128,4096]{1,0:T(8,128)(2,1)}, u32[]{:S(2)}) %copy-start) | copy-done | bytes 1048600
  2.5 0.0 copy-start.1
  2.5 0.9 copy-done.1
  3.4 0.0 copy-start.2
  3.4 0.7 copy-done.2
  4.1 93.7 %shard_map.75 = (bf16[16,4096]{1,0:T(8,128)(2,1)S(1)}, bf16[128,4096]{1,0:T(8,128)(2,1)S(1)}, f32[1,4096]{1,0:T(1,128)S(1)}, f32[1,1]{1,0:T(1,128)}) custom-call(bf16[16,4096]{1,0:T(8,128)(2,1)S(1)} %copy-done.1, bf16[128,4096]{1,0:T(8,128)(2,1)S(1)} %copy-done, f32[1,4096]{1,0:T(1,128)S(1)} %bitcast.5, s32[1,16]{1,0:T(1,128)S(1)} %bitcast.6), custom_call_target="tpu_custom_call" | custom-call | flops 1610612736 | bytes 2400000 | tf_op jit(solution)/shard_map/pallas_call | solution.py:368
  97.8 0.7 copy.12
  98.5 1.0 copy.13
  99.4 0.6 copy.14
Async XLA Ops:
  0.6 0.7 copy-start.3
  1.3 1.2 %copy-start = (bf16[128,4096]{1,0:T(8,128)(2,1)S(1)}, bf16[128,4096]{1,0:T(8,128)(2,1)}, u32[]{:S(2)}) copy-start(bf16[128,4096]{1,0:T(8,128)(2,1)} %p_hbm.1) | copy-start | bytes 3145732
  2.5 0.9 copy-start.1
  3.4 0.7 copy-start.2

commit v4 on v3

--- a/solution.py
+++ b/solution.py
@@ -20,15 +20,16 @@
 NP = 2 * PB
 NF = 4
 FC = D // NF
-SEG = D // CLASS
+PLANE = 32
+SEG = D // PLANE
 
 
 def kernel(
     q_hbm, p_hbm, gain_hbm, pos_hbm,
     qg_ref, pg_ref, gg_ref, loss_ref,
-    q_ref, p_ref, gain_ref, pos_ref,
-    qb, pb, sc, ds, dq, yr, zs, zr, dp, dps, dpr, dfin, pstat, stats, ga, gar, gb, gbr, gc, gd, et, from_y,
-    in_sem, z_r, rsy_r, dp_r, agy_r, one_s, one_r,
+    q_ref, p_ref, far_ref, gain_ref, pos_ref,
+    qb, pb, sc, ds, dq, yr, zs, zr, dp, dps, dpr, dfin, pstat, stats, ga, gar, gc, gd, et, from_y,
+    in_sem, z_r, rsy_r, dp_r, px_r, agy_r, one_s, one_r,
 ):
     dx = lax.axis_index("dx")
     dy = lax.axis_index("dy")
@@ -48,10 +49,22 @@
     yp = z * 4 + 3 - y
     pp = z * 4 + y + 1 - 2 * (y % 2)
 
-    def peer(k):
-        other = (ci + k) % CLASS
-        c2 = other // RING
-        return z_of(other % RING) * 4 + cls + c2 * (3 - 2 * cls)
+    x = dy // 4
+    z_hi = (dy // 2) % 2
+    core = dy % 2
+    plane = (x * 4 + y) * 2 + core
+    tall = z_hi * RING + z
+
+    def in_plane(k):
+        other = (plane + k) % PLANE
+        return z * 4 + (other // 2) % 4, (other // 8) * 4 + z_hi * 2 + other % 2
+
+    def along_z(k):
+        other = (tall + k) % 16
+        return (other % RING) * 4 + y, x * 4 + (other // RING) * 2 + core
+
+    def in_class(j, cc):
+        return z_of((r + j) % RING) * 4 + cls + cc * (3 - 2 * cls)
 
     def rows(block, size=QB):
         return pl.ds(pl.multiple_of(block * size, size), size)
@@ -73,13 +86,24 @@
 
     barrier = pltpu.get_barrier_semaphore()
 
-    def greet(k, _):
-        pl.semaphore_signal(barrier, inc=1, device_id=(peer(k), dy), device_id_type=MESH)
-        pl.semaphore_signal(barrier, inc=1, device_id=(dx, (dy + k) % 16), device_id_type=MESH)
-        return 0
-
-    lax.fori_loop(1, 16, greet, 0)
-    pl.semaphore_signal(barrier, inc=1, device_id=(pp, dy), device_id_type=MESH)
+    def greet(dev, other_dy):
+        pl.semaphore_signal(barrier, inc=1, device_id=(dev, other_dy), device_id_type=MESH)
+
+    def greet_plane(k, _):
+        greet(*in_plane(k))
+        return 0
+
+    def greet_z(k, _):
+        greet(*along_z(k))
+        return 0
+
+    def greet_class(k, _):
+        greet(in_class(k, 1 - c), dy)
+        return 0
+
+    lax.fori_loop(1, 16, greet_z, 0)
+    lax.fori_loop(1, RING, greet_class, 0)
+    lax.fori_loop(1, PLANE, greet_plane, 0)
 
     def embed(hidden):
         v = hidden.astype(F32)
@@ -94,7 +118,8 @@
     for f in range(NF):
         qb[f, rows(ci), :] = q_e[:, f * FC:(f + 1) * FC].astype(BF16)
 
-    pl.semaphore_wait(barrier, 31)
+    loads[3].wait()
+    pl.semaphore_wait(barrier, 31 + 15 + 7)
 
     def block(off, f, cc=None):
         return qb.at[f, rows((c if cc is None else cc) * RING + (r + off + RING) % RING), :]
@@ -119,7 +144,14 @@
         send_b(0, f).start()
         send_y(0, f).start()
 
-    loads[3].wait()
+    def swap(b):
+        return remote(p_ref.at[rows(b), :], far_ref.at[rows(b), :], one_s.at[2], px_r.at[b], pp)
+
+    def start_swap(b, _):
+        swap(b).start()
+        return 0
+
+    lax.fori_loop(0, PB // QB, start_swap, 0)
 
     def embed_block(b, _):
         e, inv_rms, inv_len = embed(p_ref[rows(b), :])
@@ -127,7 +159,13 @@
             pb[f, rows(b), :] = e[:, f * FC:(f + 1) * FC].astype(BF16)
         pstat[0, rows(b), :] = inv_rms
         pstat[1, rows(b), :] = inv_len
-        remote(pb.at[:, rows(b), :], pb.at[:, rows(b + PB // QB), :], one_s.at[2], one_r.at[2], pp).start()
+        return 0
+
+    def embed_far(b, _):
+        swap(b).wait_recv()
+        e, _, _ = embed(far_ref[rows(b), :])
+        for f in range(NF):
+            pb[f, rows(b + PB // QB), :] = e[:, f * FC:(f + 1) * FC].astype(BF16)
         return 0
 
     lax.fori_loop(0, PB // QB, embed_block, 0)
@@ -152,9 +190,8 @@
                 if h < 3 or (h == 3 and not forth):
                     send_b(h, f).start()
                 send_y(h, f).start()
-
-    swapped = pb.at[:, pl.ds(PB, PB), :]
-    remote(swapped, swapped, one_s.at[2], one_r.at[2], pp).wait_recv()
+        lax.fori_loop(max(2 * h - 3, 0), 8 if h == 4 else 2 * h - 1, embed_far, 0)
+
     for f in range(NF):
         arrived = qb.at[f, rows(1 - c, RING * QB), :]
         remote(arrived, arrived, one_s.at[1], agy_r.at[f], yp).wait_recv()
@@ -173,18 +210,17 @@
     stats[ci, 0:1, :] = top
     stats[ci, 1:2, :] = total
 
-    def to_class(ref_of, dst, i):
-        def go(k, _):
-            remote(ref_of(k), dst.at[ci], one_s.at[i], one_r.at[i], peer(k)).start()
-            return 0
-
-        lax.fori_loop(1, CLASS, go, 0)
-
-    def fifteen(ref, i):
-        part = ref.at[pl.ds(0, 15)]
+    def to_class(ref, i):
+        for j in (4, 3, 5, 2, 6, 1, 7, 0):
+            remote(ref.at[ci], ref.at[ci], one_s.at[i], one_r.at[i], in_class(j, 1 - c)).start()
+            if j:
+                remote(ref.at[ci], ref.at[ci], one_s.at[i], one_r.at[i], in_class(j, c)).start()
+
+    def several(ref, i, n):
+        part = ref.at[pl.ds(0, n)]
         return remote(part, part, one_s.at[i], one_r.at[i], pp)
 
-    to_class(lambda k: stats.at[ci], stats, 3)
+    to_class(stats, 3)
 
     offs = (4, 3, -3, 2, -2, 1, -1, 0)
     slot_after = (None, 3, 4, 5, 6, 7, 0)
@@ -197,12 +233,15 @@
     theirs = rows(1 - c, RING * QB)
     for f in range(NF):
         dq[f, theirs, :] = jnp.dot(et[theirs, :], pb[f], preferred_element_type=F32).astype(BF16)
-    for i in range(RING):
-        for f in range(NF):
-            remote(dq.at[f, dest(i, 1 - c), :], yr.at[i, f], one_s.at[4], rsy_r.at[i, f], yp).start()
-
+
+    def send_rsy(i0, i1):
+        for i in range(i0, i1):
+            for f in range(NF):
+                remote(dq.at[f, dest(i, 1 - c), :], yr.at[i, f], one_s.at[4], rsy_r.at[i, f], yp).start()
+
+    send_rsy(0, 3)
     pos_score = jnp.sum(is_pos * s_own, axis=0, keepdims=True)
-    fifteen(stats, 3).wait_recv()
+    several(stats, 3, 15).wait_recv()
     top_all = stats[0, 0:1, :]
     for k in range(1, CLASS):
         top_all = jnp.maximum(top_all, stats[k, 0:1, :])
@@ -222,19 +261,24 @@
     scale = LOGIT_SCALE * jnp.exp(stats[(1 - c) * RING + r, 0:1, :] - log_total)
     from_y[...] = jnp.transpose(jnp.broadcast_to(scale, (8, NQ)))[:, 0:1]
 
+    rest = pl.ds(FC, D - FC)
+
+    def dp_first():
+        return remote(dps.at[:, pl.ds(0, FC)], dpr.at[:, pl.ds(0, FC)], one_s.at[5], one_r.at[5], pp)
+
+    def dp_block(b):
+        return remote(dps.at[rows(b), rest], dpr.at[rows(b), rest], one_s.at[5], dp_r.at[b], pp)
+
+    def start_dp(b, _):
+        dp_block(b).start()
+        return 0
+
     for f in range(NF):
         d = LOGIT_SCALE * jnp.dot(ds[...], qb[f], preferred_element_type=F32)
         dp[:, f * FC:(f + 1) * FC] = d[0:PB, :]
         dps[:, f * FC:(f + 1) * FC] = d[PB:NP, :].astype(BF16)
-
-    def send_dp(b):
-        return remote(dps.at[rows(b), :], dpr.at[rows(b), :], one_s.at[5], dp_r.at[b], pp)
-
-    def start_dp(b, _):
-        send_dp(b).start()
-        return 0
-
-    lax.fori_loop(0, PB // QB, start_dp, 0)
+        if f == 0:
+            dp_first().start()
 
     ours = rows(c, RING * QB)
     for f in range(NF):
@@ -257,6 +301,8 @@
             after = (1 if forth else 2) if i == 0 else slot_after[i]
             remote(zs.at[i, f], zr.at[after, f], one_s.at[6], z_r.at[after, f], nxt if ahead else prv).start()
 
+    ring_step(0)
+
     prod = ds_f * sc[...]
     u = jnp.sum(prod, axis=1, keepdims=True)
     t_row = jnp.sum(prod, axis=0, keepdims=True)
@@ -275,20 +321,33 @@
             ga[f * (FC // SEG) + k, 0:1, :] = g[:, k * SEG:(k + 1) * SEG]
             ga[f * (FC // SEG) + k, 1:2, :] = jnp.broadcast_to(loss_part, (1, SEG))
 
-    to_class(lambda k: ga.at[(ci + k) % CLASS], gar, 7)
-    gar[ci] = ga[ci]
-
-    ring_step(0)
+    def to_plane(src_of, dst, i):
+        def go(k, _):
+            remote(src_of((plane + k) % PLANE), dst.at[plane], one_s.at[i], one_r.at[i], *in_plane(k)).start()
+            return 0
+
+        lax.fori_loop(1, PLANE, go, 0)
+
+    to_plane(lambda other: ga.at[other], gar, 7)
+    gar[plane] = ga[plane]
+    lax.fori_loop(0, 4, start_dp, 0)
+    send_rsy(3, 5)
     ring_step(1)
     ring_step(2)
-
-    fifteen(gar, 7).wait_recv()
+    send_rsy(5, 8)
+    lax.fori_loop(4, PB // QB, start_dp, 0)
+
+    several(gar, 7, PLANE - 1).wait_recv()
     seg = gar[0]
-    for k in range(1, CLASS):
+    for k in range(1, PLANE):
         seg = seg + gar[k]
-    gb[...] = seg
-    pair = remote(gb, gbr, one_s.at[8], one_r.at[8], pp)
-    pair.start()
+    gc[tall] = seg
+
+    def over_z(k, _):
+        remote(gc.at[tall], gc.at[tall], one_s.at[9], one_r.at[9], *along_z(k)).start()
+        return 0
+
+    lax.fori_loop(1, 16, over_z, 0)
 
     def backward(hidden, inv_rms, inv_len, d):
         g = gain_ref[...]
@@ -300,7 +359,7 @@
         return (inv_rms * (dunit - unit * mean)).astype(BF16)
 
     def p_block(b, _):
-        send_dp(b).wait_recv()
+        dp_block(b).wait_recv()
         at = rows(b)
         d = dp[at, :] + dpr[at, :].astype(F32)
         pg_ref[at, :] = backward(p_ref[at, :], pstat[0, at, :], pstat[1, at, :], d)
@@ -311,27 +370,18 @@
 
     ring_step(3)
     ring_step(4)
-
-    pair.wait_recv()
-    gc[dy] = gb[...] + gbr[...]
-
-    def over_dy(k, _):
-        remote(gc.at[dy], gc.at[dy], one_s.at[9], one_r.at[9], dx, (dy + k) % 16).start()
-        return 0
-
-    lax.fori_loop(1, 16, over_dy, 0)
+    dp_first().wait_recv()
     p_blocks(0, 2)
     ring_step(5)
     ring_step(6)
-    p_blocks(2, 4)
-
-    fifteen(gc, 9).wait_recv()
+
+    several(gc, 9, 15).wait_recv()
     seg = gc[0]
     for k in range(1, 16):
         seg = seg + gc[k]
-    gd[ci] = seg
-    to_class(lambda k: gd.at[ci], gd, 10)
-    p_blocks(4, 6)
+    gd[plane] = seg
+    to_plane(lambda other: gd.at[plane], gd, 10)
+    p_blocks(2, 6)
 
     for f in range(NF):
         rsy = remote(yr.at[RING - 1, f], yr.at[RING - 1, f], one_s.at[4], rsy_r.at[RING - 1, f], yp)
@@ -346,18 +396,18 @@
     qg_ref[...] = backward(q_ref[...], q_rms, q_len, dfin[...])
     p_blocks(6, 8)
 
-    fifteen(gd, 10).wait_recv()
-    for k in range(CLASS):
+    several(gd, 10, PLANE - 1).wait_recv()
+    for k in range(PLANE):
         gg_ref[:, k * SEG:(k + 1) * SEG] = gd[k, 0:1, :]
     loss_ref[...] = gd[0, 1:2, 0:1]
 
     for ref, i in (
-        (qb.at[:, pl.ds(0, 7 * QB), :], 0), (qb.at[:, pl.ds(0, 8 * QB), :], 1), (swapped, 2),
-        (yr, 4), (dpr, 5), (zs.at[pl.ds(0, 7)], 6), (gb, 8),
+        (qb.at[:, pl.ds(0, 7 * QB), :], 0), (qb.at[:, pl.ds(0, 8 * QB), :], 1), (far_ref, 2),
+        (yr, 4), (dpr, 5), (zs.at[pl.ds(0, 7)], 6),
     ):
         remote(ref, ref, one_s.at[i], one_r.at[i], pp).wait_send()
-    for ref, i in ((stats, 3), (gar, 7), (gc, 9), (gd, 10)):
-        fifteen(ref, i).wait_send()
+    for ref, i, n in ((stats, 3, 15), (gar, 7, PLANE - 1), (gc, 9, 15), (gd, 10, PLANE - 1)):
+        several(ref, i, n).wait_send()
 
 
 def on_device(query_hidden, passage_hidden, gain, hard_ids, positive_ids):
@@ -378,6 +428,7 @@
         scratch_shapes=[
             pltpu.VMEM((QB, D), BF16),
             pltpu.VMEM((PB, D), BF16),
+            pltpu.VMEM((PB, D), BF16),
             pltpu.VMEM((1, D), F32),
             pltpu.VMEM((1, QB), jnp.int32),
             pltpu.VMEM((NF, NQ, FC), BF16),
@@ -394,24 +445,23 @@
             pltpu.VMEM((QB, D), F32),
             pltpu.VMEM((2, PB, 1), F32),
             pltpu.VMEM((CLASS, 2, NQ), F32),
-            pltpu.VMEM((CLASS, 2, SEG), F32),
-            pltpu.VMEM((CLASS, 2, SEG), F32),
-            pltpu.VMEM((2, SEG), F32),
-            pltpu.VMEM((2, SEG), F32),
+            pltpu.VMEM((PLANE, 2, SEG), F32),
+            pltpu.VMEM((PLANE, 2, SEG), F32),
             pltpu.VMEM((16, 2, SEG), F32),
-            pltpu.VMEM((CLASS, 2, SEG), F32),
+            pltpu.VMEM((PLANE, 2, SEG), F32),
             pltpu.VMEM((NQ, NP), BF16),
             pltpu.VMEM((NQ, 1), F32),
             dma((4,)),
             dma((RING, NF)),
             dma((RING, NF)),
             dma((PB // QB,)),
+            dma((PB // QB,)),
             dma((NF,)),
             dma((11,)),
             dma((11,)),
         ],
         compiler_params=pltpu.CompilerParams(
-            collective_id=0, has_side_effects=True, vmem_limit_bytes=40 * 1024 * 1024
+            collective_id=0, has_side_effects=True, vmem_limit_bytes=60 * 1024 * 1024
         ),
         cost_estimate=pl.CostEstimate(flops=1_610_612_736, bytes_accessed=2_400_000, transcendentals=200_000),
     )(query_hidden, passage_hidden, gain.reshape(1, D), positive_ids.reshape(1, QB))

time: 102 us -> 88.4 us (0.87)
  Pallas kernels: 93.7 us -> 81.3 us
  local copies, waits for them, and re-layouts: 5.73 us -> 4.48 us
    pallas_call x1, Pallas kernels: 93.7 us -> 81.3 us  [on_device(): pl.pallas_call(kernel, out_shape=(jax.ShapeDtypeStruct((QB, D), BF16), ja...]
    unnamed x11 -> x5, local copies, waits for them, and re-layouts: 5.73 us -> 4.48 us
where the time goes in v4:
time: 88.4 us; the launch traced here: 88.2 us
  Pallas kernels  81.3 us (92%)
  local copies, waits for them, and re-layouts  4.48 us (5%)
  between operations  2.4 us (3%)
    pallas_call x1, Pallas kernels, on_device(): pl.pallas_call(kernel, out_shape=(jax.ShapeDtypeStruct((QB, D), BF16), ja...  81.3 us
    unnamed x5, local copies, waits for them, and re-layouts  4.48 us

profile of v4, /device:TPU:1, one launch (start us, length us, event | category | flops | bytes accessed | tf_op | source)
XLA Modules:
  0.0 88.2 jit_solution(18423866459553369760)
XLA Ops:
  0.6 81.3 %shard_map.75 = (bf16[16,4096]{1,0:T(8,128)(2,1)}, bf16[128,4096]{1,0:T(8,128)(2,1)}, f32[1,4096]{1,0:T(1,128)}, f32[1,1]{1,0:T(1,128)}) custom-call(bf16[16,4096]{1,0:T(8,128)(2,1)} %q_hbm.1, bf16[128,4096]{1,0:T(8,128)(2,1)} %p_hbm.1, f32[1,4096]{1,0:T(1,128)} %bitcast.5, s32[1,16]{1,0:T(1,128)} %bitcast.6), custom_call_target="tpu_custom_call" | custom-call | flops 1610612736 | bytes 2400000 | tf_op jit(solution)/shard_map/pallas_call | solution.py:418
  82.0 1.6 %copy.12 = bf16[16,4096]{1,0:T(8,128)(2,1)} copy(bf16[16,4096]{1,0:T(8,128)(2,1)} %get-tuple-element.16) | data formatting | bytes 262144
  83.5 0.0 copy-start
  83.6 2.3 %copy.13 = bf16[128,4096]{1,0:T(8,128)(2,1)} copy(bf16[128,4096]{1,0:T(8,128)(2,1)} %get-tuple-element.17) | data formatting | bytes 2097152
  85.9 0.0 copy-done
  85.9 0.6 copy.14
Async XLA Ops:
  83.5 2.3 %copy-start = (f32[1,4096]{1,0:T(1,128)S(1)}, f32[1,4096]{1,0:T(1,128)}, u32[]{:S(2)}) copy-start(f32[1,4096]{1,0:T(1,128)} %get-tuple-element.10) | copy-start | bytes 49156

commit v5 on v4

--- a/solution.py
+++ b/solution.py
@@ -20,51 +20,55 @@
 NP = 2 * PB
 NF = 4
 FC = D // NF
-PLANE = 32
-SEG = D // PLANE
+SIDE = 8
+SEG = D // SIDE
+SUB = SEG // 4
 
 
 def kernel(
     q_hbm, p_hbm, gain_hbm, pos_hbm,
     qg_ref, pg_ref, gg_ref, loss_ref,
     q_ref, p_ref, far_ref, gain_ref, pos_ref,
-    qb, pb, sc, ds, dq, yr, zs, zr, dp, dps, dpr, dfin, pstat, stats, ga, gar, gc, gd, et, from_y,
+    qb, pb, sc, ds, dq, yr, zs, zr, dp, dps, dpr, dfin, pstat, stats, ga, gar, gy, gyr, gc, gd, ge, et, from_y, qg_v, pg_v, gg_v, loss_v,
     in_sem, z_r, rsy_r, dp_r, px_r, agy_r, one_s, one_r,
 ):
     dx = lax.axis_index("dx")
     dy = lax.axis_index("dy")
-    y = dx % 4
-    z = dx // 4
-    half = z // 2
-    r = half + (z % 2) * (7 - 2 * half)
-    c = y // 2
-    cls = (y + c) % 2
+    y = dx & 3
+    z = dx >> 2
+    half = z >> 1
+    r = half + (z & 1) * (7 - 2 * half)
+    c = y >> 1
+    cls = (y + c) & 1
     ci = c * RING + r
 
     def z_of(place):
-        return 2 * place + (place // 4) * (15 - 4 * place)
-
-    nxt = z_of((r + 1) % RING) * 4 + y
-    prv = z_of((r + RING - 1) % RING) * 4 + y
+        return 2 * place + (place >> 2) * (15 - 4 * place)
+
+    nxt = z_of((r + 1) & 7) * 4 + y
+    prv = z_of((r + 7) & 7) * 4 + y
     yp = z * 4 + 3 - y
-    pp = z * 4 + y + 1 - 2 * (y % 2)
-
-    x = dy // 4
-    z_hi = (dy // 2) % 2
-    core = dy % 2
-    plane = (x * 4 + y) * 2 + core
+    pp = z * 4 + y + 1 - 2 * (y & 1)
+
+    x = dy >> 2
+    z_hi = (dy >> 1) & 1
+    core = dy & 1
+    side = x * 2 + core
     tall = z_hi * RING + z
 
-    def in_plane(k):
-        other = (plane + k) % PLANE
-        return z * 4 + (other // 2) % 4, (other // 8) * 4 + z_hi * 2 + other % 2
+    def along_side(k):
+        other = (side + k) & 7
+        return dx, (other >> 1) * 4 + z_hi * 2 + (other & 1)
+
+    def along_y(k):
+        return z * 4 + ((y + k) & 3), dy
 
     def along_z(k):
-        other = (tall + k) % 16
-        return (other % RING) * 4 + y, x * 4 + (other // RING) * 2 + core
+        other = (tall + k) & 15
+        return (other & 7) * 4 + y, x * 4 + (other >> 3) * 2 + core
 
     def in_class(j, cc):
-        return z_of((r + j) % RING) * 4 + cls + cc * (3 - 2 * cls)
+        return z_of((r + j) & 7) * 4 + cls + cc * (3 - 2 * cls)
 
     def rows(block, size=QB):
         return pl.ds(pl.multiple_of(block * size, size), size)
@@ -89,21 +93,14 @@
     def greet(dev, other_dy):
         pl.semaphore_signal(barrier, inc=1, device_id=(dev, other_dy), device_id_type=MESH)
 
-    def greet_plane(k, _):
-        greet(*in_plane(k))
-        return 0
-
-    def greet_z(k, _):
+    for k in range(1, 4):
+        greet(*along_y(k))
+    for k in range(1, RING):
+        greet(in_class(k, 1 - c), dy)
+    for k in (8, 7, 9, 6, 10, 5, 11, 4, 12, 3, 13, 2, 14, 1, 15):
         greet(*along_z(k))
-        return 0
-
-    def greet_class(k, _):
-        greet(in_class(k, 1 - c), dy)
-        return 0
-
-    lax.fori_loop(1, 16, greet_z, 0)
-    lax.fori_loop(1, RING, greet_class, 0)
-    lax.fori_loop(1, PLANE, greet_plane, 0)
+    for k in range(1, SIDE):
+        greet(*along_side(k))
 
     def embed(hidden):
         v = hidden.astype(F32)
@@ -119,10 +116,10 @@
         qb[f, rows(ci), :] = q_e[:, f * FC:(f + 1) * FC].astype(BF16)
 
     loads[3].wait()
-    pl.semaphore_wait(barrier, 31 + 15 + 7)
+    pl.semaphore_wait(barrier, 3 + 7 + 15 + 7)
 
     def block(off, f, cc=None):
-        return qb.at[f, rows((c if cc is None else cc) * RING + (r + off + RING) % RING), :]
+        return qb.at[f, rows((c if cc is None else cc) * RING + ((r + off) & 7)), :]
 
     def send_f(h, f):
         return remote(block(-h, f), block(-h, f), one_s.at[0], z_r.at[2 * h, f], nxt)
@@ -139,19 +136,17 @@
     def send_y(off, f):
         return remote(block(off, f), block(off, f), one_s.at[1], agy_r.at[f], yp)
 
+    def swap(b):
+        return remote(p_ref.at[rows(b), :], far_ref.at[rows(b), :], one_s.at[2], px_r.at[b], pp)
+
+    swap(0).start()
+    swap(1).start()
     for f in range(NF):
         send_f(0, f).start()
         send_b(0, f).start()
         send_y(0, f).start()
-
-    def swap(b):
-        return remote(p_ref.at[rows(b), :], far_ref.at[rows(b), :], one_s.at[2], px_r.at[b], pp)
-
-    def start_swap(b, _):
+    for b in range(2, PB // QB):
         swap(b).start()
-        return 0
-
-    lax.fori_loop(0, PB // QB, start_swap, 0)
 
     def embed_block(b, _):
         e, inv_rms, inv_len = embed(p_ref[rows(b), :])
@@ -226,7 +221,7 @@
     slot_after = (None, 3, 4, 5, 6, 7, 0)
 
     def dest(i, cc):
-        return rows(cc * RING + (r + offs[i] + RING) % RING)
+        return rows(cc * RING + ((r + offs[i]) & 7))
 
     et[:, 0:PB] = jnp.transpose(e_own).astype(BF16)
     et[:, PB:NP] = jnp.transpose(e_far).astype(BF16)
@@ -257,10 +252,6 @@
     ds[0:PB, :] = (weights * jnp.exp(s_own - log_total) - is_pos).astype(BF16)
     ds[PB:NP, :] = jnp.exp(s_far - log_total).astype(BF16)
     ds_f = ds[...].astype(F32)
-    et[...] = jnp.transpose(ds_f).astype(BF16)
-    scale = LOGIT_SCALE * jnp.exp(stats[(1 - c) * RING + r, 0:1, :] - log_total)
-    from_y[...] = jnp.transpose(jnp.broadcast_to(scale, (8, NQ)))[:, 0:1]
-
     rest = pl.ds(FC, D - FC)
 
     def dp_first():
@@ -280,6 +271,9 @@
         if f == 0:
             dp_first().start()
 
+    et[...] = jnp.transpose(ds_f).astype(BF16)
+    scale = LOGIT_SCALE * jnp.exp(stats[(1 - c) * RING + r, 0:1, :] - log_total)
+    from_y[...] = jnp.transpose(jnp.broadcast_to(scale, (8, NQ)))[:, 0:1]
     ours = rows(c, RING * QB)
     for f in range(NF):
         dq[f, ours, :] = (LOGIT_SCALE * jnp.dot(et[ours, :], pb[f], preferred_element_type=F32)).astype(BF16)
@@ -321,33 +315,35 @@
             ga[f * (FC // SEG) + k, 0:1, :] = g[:, k * SEG:(k + 1) * SEG]
             ga[f * (FC // SEG) + k, 1:2, :] = jnp.broadcast_to(loss_part, (1, SEG))
 
-    def to_plane(src_of, dst, i):
-        def go(k, _):
-            remote(src_of((plane + k) % PLANE), dst.at[plane], one_s.at[i], one_r.at[i], *in_plane(k)).start()
-            return 0
-
-        lax.fori_loop(1, PLANE, go, 0)
-
-    to_plane(lambda other: ga.at[other], gar, 7)
-    gar[plane] = ga[plane]
+    def spread(n, to, src_of, dst, i, order=None):
+        for k in order or range(1, n):
+            dev, other_dy = to(k)
+            remote(src_of(k), dst, one_s.at[i], one_r.at[i], dev, other_dy).start()
+
+    def total_of(ref, n):
+        out = ref[0]
+        for k in range(1, n):
+            out = out + ref[k]
+        return out
+
+    spread(SIDE, along_side, lambda k: ga.at[(side + k) & 7], gar.at[side], 7)
+    gar[side] = ga[side]
     lax.fori_loop(0, 4, start_dp, 0)
     send_rsy(3, 5)
     ring_step(1)
+    several(gar, 7, SIDE - 1).wait_recv()
+    seg = total_of(gar, SIDE)
+    for k in range(4):
+        gy[k] = seg[:, k * SUB:(k + 1) * SUB]
+    spread(4, along_y, lambda k: gy.at[(y + k) & 3], gyr.at[y], 8)
+    gyr[y] = gy[y]
     ring_step(2)
     send_rsy(5, 8)
     lax.fori_loop(4, PB // QB, start_dp, 0)
 
-    several(gar, 7, PLANE - 1).wait_recv()
-    seg = gar[0]
-    for k in range(1, PLANE):
-        seg = seg + gar[k]
-    gc[tall] = seg
-
-    def over_z(k, _):
-        remote(gc.at[tall], gc.at[tall], one_s.at[9], one_r.at[9], *along_z(k)).start()
-        return 0
-
-    lax.fori_loop(1, 16, over_z, 0)
+    several(gyr, 8, 3).wait_recv()
+    gc[tall] = total_of(gyr, 4)
+    spread(16, along_z, lambda k: gc.at[tall], gc.at[tall], 9, (8, 7, 9, 6, 10, 5, 11, 4, 12, 3, 13, 2, 14, 1, 15))
 
     def backward(hidden, inv_rms, inv_len, d):
         g = gain_ref[...]
@@ -362,7 +358,8 @@
         dp_block(b).wait_recv()
         at = rows(b)
         d = dp[at, :] + dpr[at, :].astype(F32)
-        pg_ref[at, :] = backward(p_ref[at, :], pstat[0, at, :], pstat[1, at, :], d)
+        pg_v[at, :] = backward(p_ref[at, :], pstat[0, at, :], pstat[1, at, :], d)
+        pltpu.make_async_copy(pg_v.at[at, :], pg_ref.at[at, :], in_sem.at[3]).start()
         return 0
 
     def p_blocks(b0, b1):
@@ -372,15 +369,15 @@
     ring_step(4)
     dp_first().wait_recv()
     p_blocks(0, 2)
+    several(gc, 9, 15).wait_recv()
+    gd[y] = total_of(gc, 16)
+    spread(4, along_y, lambda k: gd.at[y], gd.at[y], 10)
     ring_step(5)
     ring_step(6)
-
-    several(gc, 9, 15).wait_recv()
-    seg = gc[0]
-    for k in range(1, 16):
-        seg = seg + gc[k]
-    gd[plane] = seg
-    to_plane(lambda other: gd.at[plane], gd, 10)
+    several(gd, 10, 3).wait_recv()
+    for k in range(4):
+        ge[side, :, k * SUB:(k + 1) * SUB] = gd[k]
+    spread(SIDE, along_side, lambda k: ge.at[side], ge.at[side], 11)
     p_blocks(2, 6)
 
     for f in range(NF):
@@ -393,38 +390,61 @@
             + (zr[7, f].astype(F32) + zr[0, f].astype(F32))
         )
     _, q_rms, q_len = embed(q_ref[...])
-    qg_ref[...] = backward(q_ref[...], q_rms, q_len, dfin[...])
+    qg_v[...] = backward(q_ref[...], q_rms, q_len, dfin[...])
     p_blocks(6, 8)
 
-    several(gd, 10, PLANE - 1).wait_recv()
-    for k in range(PLANE):
-        gg_ref[:, k * SEG:(k + 1) * SEG] = gd[k, 0:1, :]
-    loss_ref[...] = gd[0, 1:2, 0:1]
+    several(ge, 11, SIDE - 1).wait_recv()
+    for k in range(SIDE):
+        gg_v[:, k * SEG:(k + 1) * SEG] = ge[k, 0:1, :]
+    loss_v[...] = ge[0, 1:2, 0:1]
+    stores = [
+        pltpu.make_async_copy(src, dst, in_sem.at[i])
+        for i, (src, dst) in enumerate(((qg_v, qg_ref), (gg_v, gg_ref), (loss_v, loss_ref)))
+    ]
+    for store in stores:
+        store.start()
+    for store in stores:
+        store.wait()
+    pltpu.make_async_copy(pg_v, pg_ref, in_sem.at[3]).wait()
 
     for ref, i in (
         (qb.at[:, pl.ds(0, 7 * QB), :], 0), (qb.at[:, pl.ds(0, 8 * QB), :], 1), (far_ref, 2),
         (yr, 4), (dpr, 5), (zs.at[pl.ds(0, 7)], 6),
     ):
         remote(ref, ref, one_s.at[i], one_r.at[i], pp).wait_send()
-    for ref, i, n in ((stats, 3, 15), (gar, 7, PLANE - 1), (gc, 9, 15), (gd, 10, PLANE - 1)):
+    for ref, i, n in (
+        (stats, 3, 15), (gar, 7, SIDE - 1), (gyr, 8, 3), (gc, 9, 15), (gd, 10, 3), (ge, 11, SIDE - 1)
+    ):
         several(ref, i, n).wait_send()
+
+
+def hand_over(qg_in, pg_in, gg_in, qg_ref, pg_ref, gg_ref, sems):
+    part = PB // 4
+    copies = [pltpu.make_async_copy(qg_in, qg_ref, sems.at[0]), pltpu.make_async_copy(gg_in, gg_ref, sems.at[1])]
+    for i in range(4):
+        at = pl.ds(i * part, part)
+        copies.append(pltpu.make_async_copy(pg_in.at[at, :], pg_ref.at[at, :], sems.at[2 + i]))
+    for copy in copies:
+        copy.start()
+    for copy in copies:
+        copy.wait()
 
 
 def on_device(query_hidden, passage_hidden, gain, hard_ids, positive_ids):
     del hard_ids
-    vmem = pl.BlockSpec(memory_space=pltpu.VMEM)
     hbm = pl.BlockSpec(memory_space=pltpu.HBM)
+    any_space = pl.BlockSpec(memory_space=pl.ANY)
     dma = pltpu.SemaphoreType.DMA
+    shapes = (
+        jax.ShapeDtypeStruct((QB, D), BF16),
+        jax.ShapeDtypeStruct((PB, D), BF16),
+        jax.ShapeDtypeStruct((1, D), F32),
+    )
     query_grad, passage_grad, gain_grad, loss = pl.pallas_call(
         kernel,
-        out_shape=(
-            jax.ShapeDtypeStruct((QB, D), BF16),
-            jax.ShapeDtypeStruct((PB, D), BF16),
-            jax.ShapeDtypeStruct((1, D), F32),
-            jax.ShapeDtypeStruct((1, 1), F32),
-        ),
+        out_shape=(*shapes, jax.ShapeDtypeStruct((1, 1), F32)),
         in_specs=[hbm] * 4,
-        out_specs=(vmem,) * 4,
+        out_specs=(any_space,) * 4,
         scratch_shapes=[
             pltpu.VMEM((QB, D), BF16),
             pltpu.VMEM((PB, D), BF16),
@@ -445,26 +465,41 @@
             pltpu.VMEM((QB, D), F32),
             pltpu.VMEM((2, PB, 1), F32),
             pltpu.VMEM((CLASS, 2, NQ), F32),
-            pltpu.VMEM((PLANE, 2, SEG), F32),
-            pltpu.VMEM((PLANE, 2, SEG), F32),
-            pltpu.VMEM((16, 2, SEG), F32),
-            pltpu.VMEM((PLANE, 2, SEG), F32),
+            pltpu.VMEM((SIDE, 2, SEG), F32),
+            pltpu.VMEM((SIDE, 2, SEG), F32),
+            pltpu.VMEM((4, 2, SUB), F32),
+            pltpu.VMEM((4, 2, SUB), F32),
+            pltpu.VMEM((16, 2, SUB), F32),
+            pltpu.VMEM((4, 2, SUB), F32),
+            pltpu.VMEM((SIDE, 2, SEG), F32),
             pltpu.VMEM((NQ, NP), BF16),
             pltpu.VMEM((NQ, 1), F32),
+            pltpu.VMEM((QB, D), BF16),
+            pltpu.VMEM((PB, D), BF16),
+            pltpu.VMEM((1, D), F32),
+            pltpu.VMEM((1, 1), F32),
             dma((4,)),
             dma((RING, NF)),
             dma((RING, NF)),
             dma((PB // QB,)),
             dma((PB // QB,)),
             dma((NF,)),
-            dma((11,)),
-            dma((11,)),
+            dma((12,)),
+            dma((12,)),
         ],
         compiler_params=pltpu.CompilerParams(
             collective_id=0, has_side_effects=True, vmem_limit_bytes=60 * 1024 * 1024
         ),
         cost_estimate=pl.CostEstimate(flops=1_610_612_736, bytes_accessed=2_400_000, transcendentals=200_000),
     )(query_hidden, passage_hidden, gain.reshape(1, D), positive_ids.reshape(1, QB))
+    query_grad, passage_grad, gain_grad = pl.pallas_call(
+        hand_over,
+        out_shape=shapes,
+        in_specs=[any_space] * 3,
+        out_specs=(any_space,) * 3,
+        scratch_shapes=[dma((6,))],
+        compiler_params=pltpu.CompilerParams(vmem_limit_bytes=60 * 1024 * 1024),
+    )(query_grad, passage_grad, gain_grad)
     return query_grad, passage_grad, gain_grad.reshape(D), loss.reshape(())
 
 

time: 88.4 us -> 125 us (1.41)
  Pallas kernels: 81.3 us -> 123 us
  local copies, waits for them, and re-layouts: 4.48 us -> 0 us
    pallas_call x1 -> x2, Pallas kernels: 81.3 us -> 123 us  [the longest x1 85.1 us: on_device(): pl.pallas_call(kernel, out_shape=(*shapes, jax.ShapeDtypeStruct((1, 1), F...]
    unnamed x5 -> x0, local copies, waits for them, and re-layouts: 4.48 us -> none
where the time goes in v5:
time: 125 us
  Pallas kernels  123 us (98%)
  between operations  2.4 us (2%)
    pallas_call x1, Pallas kernels, on_device(): pl.pallas_call(kernel, out_shape=(*shapes, jax.ShapeDtypeStruct((1, 1), F...  85.1 us
    pallas_call x1, Pallas kernels, on_device(): pl.pallas_call(hand_over, out_shape=shapes, in_specs=[any_space] * 3, out...  37.4 us

profile of v5, /device:TPU:1, one launch (start us, length us, event | category | flops | bytes accessed | tf_op | source)
XLA Modules:
  0.0 124.9 jit_solution(14502307404421775841)
XLA Ops:
  0.6 85.1 %shard_map.75 = (bf16[16,4096]{1,0:T(8,128)(2,1)}, bf16[128,4096]{1,0:T(8,128)(2,1)}, f32[1,4096]{1,0:T(1,128)}, f32[1,1]{1,0:T(1,128)}) custom-call(bf16[16,4096]{1,0:T(8,128)(2,1)} %q_hbm.1, bf16[128,4096]{1,0:T(8,128)(2,1)} %p_hbm.1, f32[1,4096]{1,0:T(1,128)} %bitcast.4, s32[1,16]{1,0:T(1,128)} %bitcast.6), custom_call_target="tpu_custom_call" | custom-call | flops 1610612736 | bytes 2400000 | tf_op jit(solution)/shard_map/pallas_call | solution.py:443
  85.8 37.4 %shard_map.76 = (bf16[16,4096]{1,0:T(8,128)(2,1)}, bf16[128,4096]{1,0:T(8,128)(2,1)}, f32[1,4096]{1,0:T(1,128)}) custom-call(bf16[16,4096]{1,0:T(8,128)(2,1)} %get-tuple-element.11.qg_in, bf16[128,4096]{1,0:T(8,128)(2,1)} %get-tuple-element.12.pg_in, f32[1,4096]{1,0:T(1,128)} %get-tuple-element.13.gg_in), custom_call_target="tpu_custom_call" | custom-call | tf_op jit(solution)/shard_map/pallas_call | solution.py:495

commit v6 on v5

--- a/solution.py
+++ b/solution.py
@@ -20,16 +20,15 @@
 NP = 2 * PB
 NF = 4
 FC = D // NF
-SIDE = 8
-SEG = D // SIDE
-SUB = SEG // 4
+PLANE = 32
+SEG = D // PLANE
 
 
 def kernel(
     q_hbm, p_hbm, gain_hbm, pos_hbm,
     qg_ref, pg_ref, gg_ref, loss_ref,
     q_ref, p_ref, far_ref, gain_ref, pos_ref,
-    qb, pb, sc, ds, dq, yr, zs, zr, dp, dps, dpr, dfin, pstat, stats, ga, gar, gy, gyr, gc, gd, ge, et, from_y, qg_v, pg_v, gg_v, loss_v,
+    qb, pb, sc, ds, dq, yr, zs, zr, dp, dps, dpr, dfin, pstat, stats, ga, gar, gc, gd, et, from_y, qg_v, pg_v, gg_v, loss_v,
     in_sem, z_r, rsy_r, dp_r, px_r, agy_r, one_s, one_r,
 ):
     dx = lax.axis_index("dx")
@@ -53,15 +52,12 @@
     x = dy >> 2
     z_hi = (dy >> 1) & 1
     core = dy & 1
-    side = x * 2 + core
+    plane = (x * 2 + core) * 4 + y
     tall = z_hi * RING + z
 
-    def along_side(k):
-        other = (side + k) & 7
-        return dx, (other >> 1) * 4 + z_hi * 2 + (other & 1)
-
-    def along_y(k):
-        return z * 4 + ((y + k) & 3), dy
+    def in_plane(k):
+        other = (plane + k) & 31
+        return z * 4 + (other & 3), (other >> 3) * 4 + z_hi * 2 + ((other >> 2) & 1)
 
     def along_z(k):
         other = (tall + k) & 15
@@ -93,14 +89,12 @@
     def greet(dev, other_dy):
         pl.semaphore_signal(barrier, inc=1, device_id=(dev, other_dy), device_id_type=MESH)
 
-    for k in range(1, 4):
-        greet(*along_y(k))
     for k in range(1, RING):
         greet(in_class(k, 1 - c), dy)
     for k in (8, 7, 9, 6, 10, 5, 11, 4, 12, 3, 13, 2, 14, 1, 15):
         greet(*along_z(k))
-    for k in range(1, SIDE):
-        greet(*along_side(k))
+    for k in range(1, PLANE):
+        greet(*in_plane(k))
 
     def embed(hidden):
         v = hidden.astype(F32)
@@ -116,7 +110,7 @@
         qb[f, rows(ci), :] = q_e[:, f * FC:(f + 1) * FC].astype(BF16)
 
     loads[3].wait()
-    pl.semaphore_wait(barrier, 3 + 7 + 15 + 7)
+    pl.semaphore_wait(barrier, 7 + 15 + 31)
 
     def block(off, f, cc=None):
         return qb.at[f, rows((c if cc is None else cc) * RING + ((r + off) & 7)), :]
@@ -270,6 +264,7 @@
         dps[:, f * FC:(f + 1) * FC] = d[PB:NP, :].astype(BF16)
         if f == 0:
             dp_first().start()
+    lax.fori_loop(0, 2, start_dp, 0)
 
     et[...] = jnp.transpose(ds_f).astype(BF16)
     scale = LOGIT_SCALE * jnp.exp(stats[(1 - c) * RING + r, 0:1, :] - log_total)
@@ -326,23 +321,17 @@
             out = out + ref[k]
         return out
 
-    spread(SIDE, along_side, lambda k: ga.at[(side + k) & 7], gar.at[side], 7)
-    gar[side] = ga[side]
-    lax.fori_loop(0, 4, start_dp, 0)
+    spread(PLANE, in_plane, lambda k: ga.at[(plane + k) & 31], gar.at[plane], 7)
+    gar[plane] = ga[plane]
+    lax.fori_loop(2, 4, start_dp, 0)
     send_rsy(3, 5)
     ring_step(1)
-    several(gar, 7, SIDE - 1).wait_recv()
-    seg = total_of(gar, SIDE)
-    for k in range(4):
-        gy[k] = seg[:, k * SUB:(k + 1) * SUB]
-    spread(4, along_y, lambda k: gy.at[(y + k) & 3], gyr.at[y], 8)
-    gyr[y] = gy[y]
     ring_step(2)
     send_rsy(5, 8)
     lax.fori_loop(4, PB // QB, start_dp, 0)
 
-    several(gyr, 8, 3).wait_recv()
-    gc[tall] = total_of(gyr, 4)
+    several(gar, 7, PLANE - 1).wait_recv()
+    gc[tall] = total_of(gar, PLANE)
     spread(16, along_z, lambda k: gc.at[tall], gc.at[tall], 9, (8, 7, 9, 6, 10, 5, 11, 4, 12, 3, 13, 2, 14, 1, 15))
 
     def backward(hidden, inv_rms, inv_len, d):
@@ -370,14 +359,10 @@
     dp_first().wait_recv()
     p_blocks(0, 2)
     several(gc, 9, 15).wait_recv()
-    gd[y] = total_of(gc, 16)
-    spread(4, along_y, lambda k: gd.at[y], gd.at[y], 10)
+    gd[plane] = total_of(gc, 16)
+    spread(PLANE, in_plane, lambda k: gd.at[plane], gd.at[plane], 10)
     ring_step(5)
     ring_step(6)
-    several(gd, 10, 3).wait_recv()
-    for k in range(4):
-        ge[side, :, k * SUB:(k + 1) * SUB] = gd[k]
-    spread(SIDE, along_side, lambda k: ge.at[side], ge.at[side], 11)
     p_blocks(2, 6)
 
     for f in range(NF):
@@ -393,10 +378,10 @@
     qg_v[...] = backward(q_ref[...], q_rms, q_len, dfin[...])
     p_blocks(6, 8)
 
-    several(ge, 11, SIDE - 1).wait_recv()
-    for k in range(SIDE):
-        gg_v[:, k * SEG:(k + 1) * SEG] = ge[k, 0:1, :]
-    loss_v[...] = ge[0, 1:2, 0:1]
+    several(gd, 10, PLANE - 1).wait_recv()
+    for k in range(PLANE):
+        gg_v[:, k * SEG:(k + 1) * SEG] = gd[k, 0:1, :]
+    loss_v[...] = gd[0, 1:2, 0:1]
     stores = [
         pltpu.make_async_copy(src, dst, in_sem.at[i])
         for i, (src, dst) in enumerate(((qg_v, qg_ref), (gg_v, gg_ref), (loss_v, loss_ref)))
@@ -413,21 +398,25 @@
     ):
         remote(ref, ref, one_s.at[i], one_r.at[i], pp).wait_send()
     for ref, i, n in (
-        (stats, 3, 15), (gar, 7, SIDE - 1), (gyr, 8, 3), (gc, 9, 15), (gd, 10, 3), (ge, 11, SIDE - 1)
+        (stats, 3, 15), (gar, 7, PLANE - 1), (gc, 9, 15), (gd, 10, PLANE - 1)
     ):
         several(ref, i, n).wait_send()
 
 
-def hand_over(qg_in, pg_in, gg_in, qg_ref, pg_ref, gg_ref, sems):
-    part = PB // 4
-    copies = [pltpu.make_async_copy(qg_in, qg_ref, sems.at[0]), pltpu.make_async_copy(gg_in, gg_ref, sems.at[1])]
+def hand_over(qg_in, pg_in, gg_in, qg_ref, pg_ref, gg_ref, qg_v, pg_v, gg_v, in_sem, out_sem):
+    parts = [(qg_in, qg_v, qg_ref), (gg_in, gg_v, gg_ref)]
     for i in range(4):
-        at = pl.ds(i * part, part)
-        copies.append(pltpu.make_async_copy(pg_in.at[at, :], pg_ref.at[at, :], sems.at[2 + i]))
-    for copy in copies:
-        copy.start()
-    for copy in copies:
-        copy.wait()
+        at = pl.ds(i * PB // 4, PB // 4)
+        parts.append(tuple(ref.at[at, :] for ref in (pg_in, pg_v, pg_ref)))
+    loads = [pltpu.make_async_copy(a, b, in_sem.at[i]) for i, (a, b, _) in enumerate(parts)]
+    stores = [pltpu.make_async_copy(b, c, out_sem.at[i]) for i, (_, b, c) in enumerate(parts)]
+    for load in loads:
+        load.start()
+    for load, store in zip(loads, stores):
+        load.wait()
+        store.start()
+    for store in stores:
+        store.wait()
 
 
 def on_device(query_hidden, passage_hidden, gain, hard_ids, positive_ids):
@@ -465,13 +454,10 @@
             pltpu.VMEM((QB, D), F32),
             pltpu.VMEM((2, PB, 1), F32),
             pltpu.VMEM((CLASS, 2, NQ), F32),
-            pltpu.VMEM((SIDE, 2, SEG), F32),
-            pltpu.VMEM((SIDE, 2, SEG), F32),
-            pltpu.VMEM((4, 2, SUB), F32),
-            pltpu.VMEM((4, 2, SUB), F32),
-            pltpu.VMEM((16, 2, SUB), F32),
-            pltpu.VMEM((4, 2, SUB), F32),
-            pltpu.VMEM((SIDE, 2, SEG), F32),
+            pltpu.VMEM((PLANE, 2, SEG), F32),
+            pltpu.VMEM((PLANE, 2, SEG), F32),
+            pltpu.VMEM((16, 2, SEG), F32),
+            pltpu.VMEM((PLANE, 2, SEG), F32),
             pltpu.VMEM((NQ, NP), BF16),
             pltpu.VMEM((NQ, 1), F32),
             pltpu.VMEM((QB, D), BF16),
@@ -497,7 +483,9 @@
         out_shape=shapes,
         in_specs=[any_space] * 3,
         out_specs=(any_space,) * 3,
-        scratch_shapes=[dma((6,))],
+        scratch_shapes=[
+            pltpu.VMEM((QB, D), BF16), pltpu.VMEM((PB, D), BF16), pltpu.VMEM((1, D), F32), dma((6,)), dma((6,))
+        ],
         compiler_params=pltpu.CompilerParams(vmem_limit_bytes=60 * 1024 * 1024),
     )(query_grad, passage_grad, gain_grad)
     return query_grad, passage_grad, gain_grad.reshape(D), loss.reshape(())

time: 125 us -> 85.2 us (0.68)
  Pallas kernels: 123 us -> 82.6 us
    pallas_call x1, Pallas kernels: 37.4 us -> 2.1 us  [on_device(): pl.pallas_call(hand_over, out_shape=shapes, in_specs=[any_space] * 3, out...]
    pallas_call x1, Pallas kernels: 85.1 us -> 80.5 us  [on_device(): pl.pallas_call(kernel, out_shape=(*shapes, jax.ShapeDtypeStruct((1, 1), F...]
where the time goes in v6:
time: 85.2 us; the launch traced here: 85 us
  Pallas kernels  82.6 us (97%)
  between operations  2.4 us (3%)
    pallas_call x1, Pallas kernels, on_device(): pl.pallas_call(kernel, out_shape=(*shapes, jax.ShapeDtypeStruct((1, 1), F...  80.5 us
    pallas_call x1, Pallas kernels, on_device(): pl.pallas_call(hand_over, out_shape=shapes, in_specs=[any_space] * 3, out...  2.1 us

profile of v6, /device:TPU:1, one launch (start us, length us, event | category | flops | bytes accessed | tf_op | source)
XLA Modules:
  0.0 85.0 jit_solution(10482196514352724066)
XLA Ops:
  0.6 80.5 %shard_map.75 = (bf16[16,4096]{1,0:T(8,128)(2,1)}, bf16[128,4096]{1,0:T(8,128)(2,1)}, f32[1,4096]{1,0:T(1,128)}, f32[1,1]{1,0:T(1,128)}) custom-call(bf16[16,4096]{1,0:T(8,128)(2,1)} %q_hbm.1, bf16[128,4096]{1,0:T(8,128)(2,1)} %p_hbm.1, f32[1,4096]{1,0:T(1,128)} %bitcast.4, s32[1,16]{1,0:T(1,128)} %bitcast.6), custom_call_target="tpu_custom_call" | custom-call | flops 1610612736 | bytes 2400000 | tf_op jit(solution)/shard_map/pallas_call | solution.py:432
  81.1 2.1 %shard_map.76 = (bf16[16,4096]{1,0:T(8,128)(2,1)}, bf16[128,4096]{1,0:T(8,128)(2,1)}, f32[1,4096]{1,0:T(1,128)}) custom-call(bf16[16,4096]{1,0:T(8,128)(2,1)} %get-tuple-element.11.qg_in, bf16[128,4096]{1,0:T(8,128)(2,1)} %get-tuple-element.12.pg_in, f32[1,4096]{1,0:T(1,128)} %get-tuple-element.13.gg_in), custom_call_target="tpu_custom_call" | custom-call | tf_op jit(solution)/shard_map/pallas_call | solution.py:481

commit v7 on v6

--- a/solution.py
+++ b/solution.py
@@ -228,7 +228,7 @@
             for f in range(NF):
                 remote(dq.at[f, dest(i, 1 - c), :], yr.at[i, f], one_s.at[4], rsy_r.at[i, f], yp).start()
 
-    send_rsy(0, 3)
+    send_rsy(0, 2)
     pos_score = jnp.sum(is_pos * s_own, axis=0, keepdims=True)
     several(stats, 3, 15).wait_recv()
     top_all = stats[0, 0:1, :]
@@ -264,7 +264,6 @@
         dps[:, f * FC:(f + 1) * FC] = d[PB:NP, :].astype(BF16)
         if f == 0:
             dp_first().start()
-    lax.fori_loop(0, 2, start_dp, 0)
 
     et[...] = jnp.transpose(ds_f).astype(BF16)
     scale = LOGIT_SCALE * jnp.exp(stats[(1 - c) * RING + r, 0:1, :] - log_total)
@@ -323,12 +322,13 @@
 
     spread(PLANE, in_plane, lambda k: ga.at[(plane + k) & 31], gar.at[plane], 7)
     gar[plane] = ga[plane]
+    dp_block(0).start()
+    send_rsy(2, 4)
+    ring_step(1)
+    dp_block(1).start()
+    send_rsy(4, 5)
+    ring_step(2)
     lax.fori_loop(2, 4, start_dp, 0)
-    send_rsy(3, 5)
-    ring_step(1)
-    ring_step(2)
-    send_rsy(5, 8)
-    lax.fori_loop(4, PB // QB, start_dp, 0)
 
     several(gar, 7, PLANE - 1).wait_recv()
     gc[tall] = total_of(gar, PLANE)
@@ -355,13 +355,18 @@
         lax.fori_loop(b0, b1, p_block, 0)
 
     ring_step(3)
+    send_rsy(5, 7)
+    dp_block(4).start()
     ring_step(4)
+    dp_block(5).start()
     dp_first().wait_recv()
     p_blocks(0, 2)
+    ring_step(5)
     several(gc, 9, 15).wait_recv()
     gd[plane] = total_of(gc, 16)
     spread(PLANE, in_plane, lambda k: gd.at[plane], gd.at[plane], 10)
-    ring_step(5)
+    lax.fori_loop(6, 8, start_dp, 0)
+    send_rsy(7, 8)
     ring_step(6)
     p_blocks(2, 6)
 

time: 85.2 us -> 82.8 us (0.972)
  Pallas kernels: 82.6 us -> 79.8 us
    pallas_call x1, Pallas kernels: 80.5 us -> 77.7 us  [on_device(): pl.pallas_call(kernel, out_shape=(*shapes, jax.ShapeDtypeStruct((1, 1), F...]
where the time goes in v7:
time: 82.8 us; the launch traced here: 82.2 us
  Pallas kernels  79.8 us (96%)
  between operations  2.4 us (3%)
    pallas_call x1, Pallas kernels, on_device(): pl.pallas_call(kernel, out_shape=(*shapes, jax.ShapeDtypeStruct((1, 1), F...  77.7 us
    pallas_call x1, Pallas kernels, on_device(): pl.pallas_call(hand_over, out_shape=shapes, in_specs=[any_space] * 3, out...  2.1 us

profile of v7, /device:TPU:1, one launch (start us, length us, event | category | flops | bytes accessed | tf_op | source)
XLA Modules:
  0.0 82.2 jit_solution(7558496930130325116)
XLA Ops:
  0.6 77.7 %shard_map.75 = (bf16[16,4096]{1,0:T(8,128)(2,1)}, bf16[128,4096]{1,0:T(8,128)(2,1)}, f32[1,4096]{1,0:T(1,128)}, f32[1,1]{1,0:T(1,128)}) custom-call(bf16[16,4096]{1,0:T(8,128)(2,1)} %q_hbm.1, bf16[128,4096]{1,0:T(8,128)(2,1)} %p_hbm.1, f32[1,4096]{1,0:T(1,128)} %bitcast.4, s32[1,16]{1,0:T(1,128)} %bitcast.6), custom_call_target="tpu_custom_call" | custom-call | flops 1610612736 | bytes 2400000 | tf_op jit(solution)/shard_map/pallas_call | solution.py:437
  78.3 2.1 %shard_map.76 = (bf16[16,4096]{1,0:T(8,128)(2,1)}, bf16[128,4096]{1,0:T(8,128)(2,1)}, f32[1,4096]{1,0:T(1,128)}) custom-call(bf16[16,4096]{1,0:T(8,128)(2,1)} %get-tuple-element.11.qg_in, bf16[128,4096]{1,0:T(8,128)(2,1)} %get-tuple-element.12.pg_in, f32[1,4096]{1,0:T(1,128)} %get-tuple-element.13.gg_in), custom_call_target="tpu_custom_call" | custom-call | tf_op jit(solution)/shard_map/pallas_call | solution.py:486

commit v8 on v7

--- a/solution.py
+++ b/solution.py
@@ -179,7 +179,7 @@
                 if h < 3 or (h == 3 and not forth):
                     send_b(h, f).start()
                 send_y(h, f).start()
-        lax.fori_loop(max(2 * h - 3, 0), 8 if h == 4 else 2 * h - 1, embed_far, 0)
+        lax.fori_loop(max(2 * h - 4, 0), 8 if h == 4 else 2 * h - 2, embed_far, 0)
 
     for f in range(NF):
         arrived = qb.at[f, rows(1 - c, RING * QB), :]

time: 82.8 us -> 82.8 us (level)
  no operation moved by 1% of the time
where the time goes in v8:
time: 82.8 us; the launch traced here: 82.2 us
  Pallas kernels  79.8 us (96%)
  between operations  2.4 us (3%)
    pallas_call x1, Pallas kernels, on_device(): pl.pallas_call(kernel, out_shape=(*shapes, jax.ShapeDtypeStruct((1, 1), F...  77.7 us
    pallas_call x1, Pallas kernels, on_device(): pl.pallas_call(hand_over, out_shape=shapes, in_specs=[any_space] * 3, out...  2.1 us

profile of v8, /device:TPU:1, one launch (start us, length us, event | category | flops | bytes accessed | tf_op | source)
XLA Modules:
  0.0 82.2 jit_solution(13743278549246315921)
XLA Ops:
  0.6 77.7 %shard_map.75 = (bf16[16,4096]{1,0:T(8,128)(2,1)}, bf16[128,4096]{1,0:T(8,128)(2,1)}, f32[1,4096]{1,0:T(1,128)}, f32[1,1]{1,0:T(1,128)}) custom-call(bf16[16,4096]{1,0:T(8,128)(2,1)} %q_hbm.1, bf16[128,4096]{1,0:T(8,128)(2,1)} %p_hbm.1, f32[1,4096]{1,0:T(1,128)} %bitcast.4, s32[1,16]{1,0:T(1,128)} %bitcast.6), custom_call_target="tpu_custom_call" | custom-call | flops 1610612736 | bytes 2400000 | tf_op jit(solution)/shard_map/pallas_call | solution.py:437
  78.3 2.1 %shard_map.76 = (bf16[16,4096]{1,0:T(8,128)(2,1)}, bf16[128,4096]{1,0:T(8,128)(2,1)}, f32[1,4096]{1,0:T(1,128)}) custom-call(bf16[16,4096]{1,0:T(8,128)(2,1)} %get-tuple-element.11.qg_in, bf16[128,4096]{1,0:T(8,128)(2,1)} %get-tuple-element.12.pg_in, f32[1,4096]{1,0:T(1,128)} %get-tuple-element.13.gg_in), custom_call_target="tpu_custom_call" | custom-call | tf_op jit(solution)/shard_map/pallas_call | solution.py:486
